TPU v7x, 512 devices: a whole 4x8x8 slice. The times are simulated.
512 devices in a mesh: row: 16 (over z_lo, x), col: 16 (over y, z_hi), cond: 2 (over core).
Axes of the slice: x: 4, y: 8, z: 8 (z_hi: 2, z_lo: 4; z = z_hi * 4 + z_lo), core: 2. Of those that a mesh axis runs over, the one named last changes fastest.
Arguments:
- mask: float32 [2048, 2048], P('row', 'col'), may hold values from -1 to 1
- target: int32 [2048, 2048], P('row', 'col'), may hold values 0 or 1
- cond_index: int32 [4], P('cond'), may hold values from 0 to 7
- kernels: float32 [8, 2, 12, 576], replicated, may hold values from -6 to 6
- dose: float32 [8], replicated, may hold values from 0.7 to 1.4
Outputs:
- mask_grad: float32 [2048, 2048], P('row', 'col')
All inputs are finite; a program needn't handle non-finite values. No bound on the sum of `target` on one device may be relied on, other than what follows from the above.
Results may differ from a plain program's by a relative error of at most 0.0003.
Values sent between devices are 32-bit elements; how exact they have to be, the bound alone decides.
A program may use at most 64 MiB of HBM per device.

v0:
```python
import math

import jax
import jax.numpy as jnp
from jax import lax
from jax.sharding import PartitionSpec as P

MARGIN = 128
BAND = 24


STEEP = 4.0
THRESH = 0.6


def extended(block, sides, width):
    for axis, dim in sides:
        count = lax.axis_size(axis)
        forward = [(i, i + 1) for i in range(count - 1)]
        backward = [(target, source) for source, target in forward]
        low = lax.ppermute(
            lax.slice_in_dim(block, block.shape[dim] - width, None, axis=dim), axis, forward
        )
        high = lax.ppermute(lax.slice_in_dim(block, 0, width, axis=dim), axis, backward)
        block = jnp.concatenate([low, block, high], axis=dim)
    return block


def highest(left_side, right_side):
    return jnp.dot(
        left_side, right_side, precision=lax.Precision.HIGHEST, preferred_element_type=jnp.float32
    )


def tables(length, start, window_size, band_size):
    frequency = jnp.arange(band_size, dtype=jnp.int32) - band_size // 2
    positions = jnp.arange(length, dtype=jnp.int32) + start
    phases = frequency[:, None] * positions[None, :] % window_size
    angles = phases.astype(jnp.float32) * (2.0 * math.pi / window_size)
    return (jnp.cos(angles), jnp.sin(angles))


def row_product(segment, row_start, window_size, band_size):
    cosine_table, sine_table = tables(segment.shape[0], row_start, window_size, band_size)
    return highest(jnp.concatenate([cosine_table, sine_table], axis=0), segment)


def col_product(partial_rows, col_start, window_size, band_size):
    cosine_table, sine_table = tables(partial_rows.shape[1], col_start, window_size, band_size)
    products = highest(partial_rows, jnp.concatenate([cosine_table, sine_table], axis=0).T)
    upper_cos = products[:band_size, :band_size]
    upper_sin = products[:band_size, band_size:]
    lower_cos = products[band_size:, :band_size]
    lower_sin = products[band_size:, band_size:]
    return jnp.stack([upper_cos - lower_sin, -lower_cos - upper_sin]) / window_size


def tile_loss(spectrum, kernel, dose_value, goal_map):
    tile_size = goal_map.shape[0]
    band_size = spectrum.shape[1]
    window_size = tile_size + 2 * MARGIN
    kernel_real = kernel[0].reshape(-1, band_size, band_size)
    kernel_imag = kernel[1].reshape(-1, band_size, band_size)
    kernel_count = kernel_real.shape[0]
    product_real = kernel_real * spectrum[0] - kernel_imag * spectrum[1]
    product_imag = kernel_real * spectrum[1] + kernel_imag * spectrum[0]
    stacked = jnp.concatenate([product_real, product_imag], axis=1)
    stacked = jnp.transpose(stacked, (1, 0, 2)).reshape(2 * band_size, kernel_count * band_size)
    cosine_table, sine_table = tables(tile_size, MARGIN, window_size, band_size)
    cosine_cols = cosine_table.T
    sine_cols = sine_table.T
    inverse_left = jnp.concatenate(
        [
            jnp.concatenate([cosine_cols, -sine_cols], 1),
            jnp.concatenate([sine_cols, cosine_cols], 1),
        ],
        0,
    )
    partial_rows = highest(inverse_left, stacked)
    rows_real = partial_rows[:tile_size].reshape(tile_size, kernel_count, band_size)
    rows_imag = partial_rows[tile_size:].reshape(tile_size, kernel_count, band_size)
    rows_both = jnp.concatenate([rows_real, rows_imag], axis=2)
    rows_both = jnp.transpose(rows_both, (1, 0, 2)).reshape(kernel_count * tile_size, 2 * band_size)
    inverse_right = jnp.concatenate(
        [
            jnp.concatenate([cosine_table, sine_table], 1),
            jnp.concatenate([-sine_table, cosine_table], 1),
        ],
        0,
    )
    fields = highest(rows_both, inverse_right)
    squared = (fields * fields).reshape(kernel_count, tile_size, 2, tile_size)
    intensity = jnp.sum(squared, axis=(0, 2)) / (kernel_count * band_size * band_size)
    resist = jax.nn.sigmoid(STEEP * (dose_value * intensity - THRESH))
    return jnp.sum(jnp.square(resist - goal_map))


def interior_adjoint(cotangent, tile_size, window_size):
    band_size = cotangent.shape[1]
    cosine_table, sine_table = tables(tile_size, MARGIN, window_size, band_size)
    joined = jnp.concatenate([cotangent[0], cotangent[1]], axis=1)
    right_side = jnp.concatenate(
        [
            jnp.concatenate([cosine_table, -sine_table], 1),
            jnp.concatenate([-sine_table, -cosine_table], 1),
        ],
        0,
    )
    halves = highest(joined, right_side)
    stacked = jnp.concatenate([halves[:, :tile_size], halves[:, tile_size:]], axis=0)
    left_side = jnp.concatenate([cosine_table, sine_table], axis=0).T
    return highest(left_side, stacked) / window_size


def shards(mask, target, cond_index, kernels, dose):
    tile_size = mask.shape[0]
    window_size = tile_size + 2 * MARGIN
    window = extended(mask, (("row", 0), ("col", 1)), MARGIN)
    spectrum = col_product(row_product(window, 0, window_size, BAND), 0, window_size, BAND)
    goal_map = target.astype(jnp.float32)
    summed = jnp.zeros((2, BAND, BAND), jnp.float32)
    for ordinal in range(cond_index.shape[0]):
        setting = cond_index[ordinal]
        kernel = lax.dynamic_index_in_dim(kernels, setting, 0, keepdims=False)
        dose_value = lax.dynamic_index_in_dim(dose, setting, 0, keepdims=False)
        summed = summed + jax.grad(tile_loss)(spectrum, kernel, dose_value, goal_map)
    local_terms = interior_adjoint(summed, tile_size, window_size)
    return lax.psum(local_terms, "cond")


def solution(mesh):
    in_specs = (P("row", "col"), P("row", "col"), P("cond"), P(), P())
    out_specs = P("row", "col")
    return jax.shard_map(shards, mesh=mesh, in_specs=in_specs, out_specs=out_specs, check_vma=False)
```

profile of v0, /device:TPU:1, one launch (start us, length us, event | category | flops | bytes accessed | tf_op | source)
XLA Modules:
  0.0 131.9 jit_solution(18439680603129885286)
XLA Ops:
  6.5 3.9 %collective-permute-start = (f32[128,128]{1,0:T(8,128)}, f32[128,128]{1,0:T(8,128)S(1)}, u32[]{:S(2)}, u32[]{:S(2)}) collective-permute-start(f32[128,128]{1,0:T(8,128)} %param.5), channel_id=1, source_target_pairs={{0,32},{32,64},{64,96},{96,128},{128,160},{160,192},{192,224},{224... | collective-permute-start | bytes 196616 | tf_op jit(solution)/shard_map/ppermute | solution.py:21
  10.5 1.3 collective-permute-start.1
  11.8 0.2 fusion.44
  12.0 0.1 fusion.77
  12.2 1.3 %fusion.100 = (s32[1]{0:T(128)}, s32[1]{0:T(128)}) fusion(s32[2]{0:T(128)} %param.7), kind=kLoop, calls=%fused_computation.146 | loop fusion | bytes 16 | tf_op jit(solution)/shard_map/slice | solution.py:123
  17.5 1.4 %fusion.99 = (f32[1]{0:T(128)}, f32[1]{0:T(128)}) fusion(f32[8]{0:T(128)} %param.9, s32[]{:T(128)S(6)} %select_n.60, s32[]{:T(128)S(6)} %select_n.63), kind=kLoop, calls=%fused_computation.145 | loop fusion | bytes 24 | tf_op jit(solution)/shard_map/jit(dynamic_index_in_dim)/dynamic_slice | solution.py:125
  21.6 1.3 dynamic-slice_reduce_fusion.3
  22.9 0.1 squeeze.31
  23.0 0.1 squeeze.32
  23.1 0.1 squeeze.34
  23.2 0.1 squeeze.35
  23.4 0.8 constant_dynamic-update-slice_fusion.1
  24.2 10.6 %collective-permute-start.2 = (f32[384,128]{1,0:T(8,128)S(1)}, f32[384,128]{1,0:T(8,128)S(1)}, u32[]{:S(2)}, u32[]{:S(2)}) collective-permute-start(f32[384,128]{1,0:T(8,128)S(1)} %constant_dynamic-update-slice_fusion), channel_id=1, source_target_pairs={{0,2},{2,4},{4,6},{6,8},{8,10},{10,12},{12,14},{14,16},{16,18},{18... | collective-permute-start | bytes 589832 | tf_op jit(solution)/shard_map/ppermute | solution.py:21
  34.9 1.3 collective-permute-start.3
  36.2 0.1 fusion.79
  36.3 1.8 %collective-permute-done.2 = f32[384,128]{1,0:T(8,128)S(1)} collective-permute-done((f32[384,128]{1,0:T(8,128)S(1)}, f32[384,128]{1,0:T(8,128)S(1)}, u32[]{:S(2)}, u32[]{:S(2)}) %collective-permute-start.2) | collective-permute-done | bytes 196640 | tf_op jit(solution)/shard_map/ppermute | solution.py:21
  38.1 7.9 %collective-permute-done.3 = f32[384,128]{1,0:T(8,128)S(1)} collective-permute-done((f32[384,128]{1,0:T(8,128)S(1)}, f32[384,128]{1,0:T(8,128)S(1)}, u32[]{:S(2)}, u32[]{:S(2)}) %collective-permute-start.3) | collective-permute-done | bytes 196640 | tf_op jit(solution)/shard_map/ppermute | solution.py:24
  46.0 0.4 fusion.6
  46.5 0.2 fusion.32
  46.7 0.1 fusion.57
  46.8 0.1 multiply_subtract_fusion.1
  46.9 0.8 maximum_bitcast_fusion
  47.6 0.1 copy.35
  47.7 0.4 fusion.71
  48.3 2.6 %fusion.102 = (f32[1536,256]{1,0:T(8,128)}, f32[1536,256]{1,0:T(8,128)S(1)}) fusion(f32[24,128]{1,0:T(8,128)S(1)} %get-tuple-element.51, f32[24,128]{1,0:T(8,128)S(1)} %get-tuple-element.49, f32[24,128]{1,0:T(8,128)S(1)} %get-tuple-element.50, f32[6,8,12,128]{3,2,1,0:T(8,128)S(1)} %bitcast.85), kind=kOutput, calls=%fused_computation.148 | convolution fusion | flops 226922496 | bytes 3477504 | tf_op jit(solution)/shard_map/jvp()/dot_general | solution.py:30
  50.9 2.1 %reshape.142 = f32[12,128,2,128]{3,2,1,0:T(2,128)S(1)} reshape(f32[1536,256]{1,0:T(8,128)} %get-tuple-element.60) | data formatting | bytes 3145728 | tf_op jit(solution)/shard_map/jvp()/reshape | solution.py:92
  53.0 1.7 %copy.28 = f32[48,12,24]{0,2,1:T(8,128)} copy(f32[48,12,24]{2,0,1:T(8,128)} %get-tuple-element.62) | data formatting | bytes 110592 | tf_op jit(solution)/shard_map/jvp()/transpose | solution.py:68
  54.7 1.3 fusion.72
  56.1 3.1 %fusion.101 = (f32[1536,256]{1,0:T(8,128)}, f32[1536,256]{1,0:T(8,128)}) fusion(f32[24,128]{1,0:T(8,128)S(1)} %get-tuple-element.51, f32[24,128]{1,0:T(8,128)S(1)} %get-tuple-element.49, f32[24,128]{1,0:T(8,128)S(1)} %get-tuple-element.50, f32[6,8,12,128]{3,2,1,0:T(8,128)S(1)} %bitcast.86), kind=kOutput, calls=%fused_computation.147 | convolution fusion | flops 226922496 | bytes 3477504 | tf_op jit(solution)/shard_map/jvp()/dot_general | solution.py:30
  59.3 2.9 %reshape.128 = f32[12,128,2,128]{3,2,1,0:T(2,128)} reshape(f32[1536,256]{1,0:T(8,128)} %get-tuple-element.58) | data formatting | bytes 3145728 | tf_op jit(solution)/shard_map/jvp()/reshape | solution.py:92
  62.1 1.3 reduce_sum.97
  63.4 2.7 %reduce_sum.86 = f32[128,128]{1,0:T(8,128)} reduce(f32[12,128,2,128]{3,2,1,0:T(2,128)} %reshape.128, f32[]{:T(128)} %constant.70.clone.1), dimensions={0,2}, to_apply=%region_0.1 | reduce | flops 376832 | bytes 1638404 | tf_op jit(solution)/shard_map/jvp()/reduce_sum | solution.py:93
  66.1 1.6 %fusion.28 = (f32[128,128]{1,0:T(8,128)S(1)}, f32[128,128]{1,0:T(8,128)}) fusion(s32[128,128]{1,0:T(8,128)} %param.6, f32[128,128]{1,0:T(8,128)} %reduce_sum.86, f32[]{:T(128)} %bitcast.11, f32[]{:T(128)} %bitcast.10, f32[]{:T(128)} %bitcast.28, f32[128,128]{1,0:T(8,128)} %reduce_sum.97, f32[]{:T(128)} %bitcast.27), kind=kLoop, calls=%fused_computation.50 | loop fusion | flops 442368 | bytes 327696 | tf_op jit(solution)/shard_map/transpose(jvp())/div | solution.py:93
  67.7 0.5 broadcast_in_dim.4
  68.2 2.4 %fusion.2 = f32[1536,48]{0,1:T(8,128)} fusion(f32[192,8,2,128]{3,2,1,0:T(2,128)S(1)} %bitcast.81, f32[1536,256]{1,0:T(8,128)S(1)} %copy-done, f32[24,128]{1,0:T(8,128)S(1)} %get-tuple-element.51, f32[24,128]{1,0:T(8,128)S(1)} %get-tuple-element.49, f32[24,128]{1,0:T(8,128)S(1)} %get-tuple-element.50), kind=kOutput, calls=%fused_computation.4 | convolution fusion | flops 227315712 | bytes 3477504 | tf_op jit(solution)/shard_map/transpose(jvp())/dot_general | solution.py:30
  70.7 1.1 reshape.130
  71.9 0.4 fusion.22
  72.3 0.1 copy.34
  72.5 0.1 multiply_reduce_fusion.7
  72.6 0.5 broadcast_in_dim.5
  73.1 1.7 %fusion = f32[1536,48]{0,1:T(8,128)S(1)} fusion(f32[192,8,2,128]{3,2,1,0:T(2,128)S(1)} %bitcast.82, f32[1536,256]{1,0:T(8,128)S(1)} %get-tuple-element.61, f32[24,128]{1,0:T(8,128)S(1)} %get-tuple-element.51, f32[24,128]{1,0:T(8,128)S(1)} %get-tuple-element.49, f32[24,128]{1,0:T(8,128)S(1)} %get-tuple-element.50), kind=kOutput, calls=%fused_computation.1 | convolution fusion | flops 227315712 | bytes 3477504 | tf_op jit(solution)/shard_map/transpose(jvp())/dot_general | solution.py:30
  75.1 0.4 fusion.18
  75.5 0.1 copy.41
  75.6 0.1 multiply_reduce_fusion.3
  75.7 0.2 fusion.35
  76.0 0.9 convolution_multiply_fusion
  76.9 46.6 %all-reduce.14.cloned.1.call-done = f32[128,128]{1,0:T(8,128)} async-done(((f32[128,128]{1,0:T(8,128)}), f32[128,128]{1,0:T(8,128)}) %all-reduce.14.cloned.1.call-update) | async-done | bytes 65552 | tf_op jit(solution)/shard_map/psum | solution.py:128
  123.6 1.5 %copy.71 = f32[128,128]{1,0:T(8,128)} copy(f32[128,128]{1,0:T(8,128)} %all-reduce.14.cloned.1.call-done) | data formatting | bytes 131072
  (40 shorter events, 0.7 us)
Async XLA Ops:
  6.5 117.0 %all-reduce.14.cloned.1.call-start = ((), (), s32[]{:S(2)}) async-start(), calls=%async_computation | async-start | bytes 131072 | tf_op jit(solution)/shard_map/psum | solution.py:128
  6.5 16.8 %collective-permute-start = (f32[128,128]{1,0:T(8,128)}, f32[128,128]{1,0:T(8,128)S(1)}, u32[]{:S(2)}, u32[]{:S(2)}) collective-permute-start(f32[128,128]{1,0:T(8,128)} %param.5), channel_id=1, source_target_pairs={{0,32},{32,64},{64,96},{96,128},{128,160},{160,192},{192,224},{224... | collective-permute-start | bytes 196616 | tf_op jit(solution)/shard_map/ppermute | solution.py:21
  10.5 13.7 %collective-permute-start.1 = (f32[128,128]{1,0:T(8,128)}, f32[128,128]{1,0:T(8,128)S(1)}, u32[]{:S(2)}, u32[]{:S(2)}) collective-permute-start(f32[128,128]{1,0:T(8,128)} %param.5), channel_id=1, source_target_pairs={{32,0},{64,32},{96,64},{128,96},{160,128},{192,160},{224,192},{256... | collective-permute-start | bytes 196616 | tf_op jit(solution)/shard_map/ppermute | solution.py:24
  23.0 23.9 %copy-start.1 = (f32[12,24,24]{2,1,0:T(8,128)}, f32[12,24,24]{2,1,0:T(8,128)S(1)}, u32[]{:S(2)}) copy-start(f32[12,24,24]{2,1,0:T(8,128)S(1)} %squeeze.31) | copy-start | bytes 82948
  23.1 23.8 %copy-start.3 = (f32[12,24,24]{2,1,0:T(8,128)}, f32[12,24,24]{2,1,0:T(8,128)S(1)}, u32[]{:S(2)}) copy-start(f32[12,24,24]{2,1,0:T(8,128)S(1)} %squeeze.32) | copy-start | bytes 82948
  24.2 13.9 %collective-permute-start.2 = (f32[384,128]{1,0:T(8,128)S(1)}, f32[384,128]{1,0:T(8,128)S(1)}, u32[]{:S(2)}, u32[]{:S(2)}) collective-permute-start(f32[384,128]{1,0:T(8,128)S(1)} %constant_dynamic-update-slice_fusion), channel_id=1, source_target_pairs={{0,2},{2,4},{4,6},{6,8},{8,10},{10,12},{12,14},{14,16},{16,18},{18... | collective-permute-start | bytes 589832 | tf_op jit(solution)/shard_map/ppermute | solution.py:21
  34.9 11.1 %collective-permute-start.3 = (f32[384,128]{1,0:T(8,128)S(1)}, f32[384,128]{1,0:T(8,128)S(1)}, u32[]{:S(2)}, u32[]{:S(2)}) collective-permute-start(f32[384,128]{1,0:T(8,128)S(1)} %constant_dynamic-update-slice_fusion), channel_id=1, source_target_pairs={{2,0},{4,2},{6,4},{8,6},{10,8},{12,10},{14,12},{16,14},{18,16},{20... | collective-permute-start | bytes 589832 | tf_op jit(solution)/shard_map/ppermute | solution.py:24
  63.4 4.8 %copy-start = (f32[1536,256]{1,0:T(8,128)S(1)}, f32[1536,256]{1,0:T(8,128)}, u32[]{:S(2)}) copy-start(f32[1536,256]{1,0:T(8,128)} %get-tuple-element.59) | copy-start | bytes 4718596
  70.7 1.8 %copy-start.2 = (f32[12,24,24]{2,1,0:T(8,128)S(1)}, f32[12,24,24]{2,1,0:T(8,128)}, u32[]{:S(2)}) copy-start(f32[12,24,24]{2,1,0:T(8,128)} %copy-done.1) | copy-start | bytes 82948
  70.7 1.8 %copy-start.4 = (f32[12,24,24]{2,1,0:T(8,128)S(1)}, f32[12,24,24]{2,1,0:T(8,128)}, u32[]{:S(2)}) copy-start(f32[12,24,24]{2,1,0:T(8,128)} %copy-done.3) | copy-start | bytes 82948
  71.8 0.8 copy-start.5
Sparse Core Ops, SparseCore 0:
  77.0 46.4 all-reduce.13
where the time goes:
time: 133 us; the launch traced here: 132 us
  waiting for transfers between devices  56.4 us (42%)
  between operations  20.5 us (15%)
  starting transfers between devices  17.2 us (13%)
  local copies, waits for them, and re-layouts  16.5 us (12%)
  matrix products  14.1 us (11%)
  other arithmetic  7.17 us (5%)
    psum x1, waiting for transfers between devices, shards(): return lax.psum(local_terms, 'cond')  46.6 us
    ppermute x2, starting transfers between devices, extended(): lax.ppermute(lax.slice_in_dim(block, block.shape[dim] - width, None, axis...  14.6 us
    dot_general x12, matrix products, highest(): jnp.dot(left_side, right_side, precision=lax.Precision.HIGHEST, preferred...  14.1 us
    ppermute x2, waiting for transfers between devices, extended(): lax.ppermute(lax.slice_in_dim(block, 0, width, axis=dim), axis, backward)  7.92 us
    reshape x2, local copies, waits for them, and re-layouts, tile_loss(): squared = (fields * fields).reshape(kernel_count, tile_size, 2, tile_size)  4.94 us
    reduce_sum x2, other arithmetic, tile_loss(): jnp.sum(squared, axis=(0, 2)) / (kernel_count * band_size * band_size)  3.94 us
  transfers between devices with their start and end apart: 5, of which 3 were waited for; matrix products, arithmetic and copies ran while one was open for 4% of the time, Pallas kernels for 0%

commit v1 on v0

v1 whole, which is shorter than its diff:
```python
import functools
import math

import jax
import jax.numpy as jnp
import ml_dtypes
import numpy as np
from jax import lax
from jax.experimental import pallas as pl
from jax.experimental.pallas import tpu as pltpu
from jax.sharding import PartitionSpec as P

MESH = pl.DeviceIdType.MESH
BF = jnp.bfloat16
F32 = jnp.float32

TILE = 128
MARGIN = 128
WINDOW = TILE + 2 * MARGIN
BAND = 24
KERNELS = 12
HALF = BAND // 2
REAL = 2 * HALF + 1
PACK = 5
GRID = 48
GROUP = 4
CONDS = 2
TILES = CONDS * KERNELS // GROUP
STEEP = 4.0
THRESH = 0.6
OFFSETS = [(-1, -1), (-1, 0), (-1, 1), (0, -1), (0, 1), (1, -1), (1, 0), (1, 1)]
FREQ = np.arange(BAND) - HALF
UNIT = 2.0 * math.pi / WINDOW


def parts(table):
    high = table.astype(ml_dtypes.bfloat16)
    low = (table - high.astype(np.float64)).astype(ml_dtypes.bfloat16)
    return high, low


def left3(table):
    high, low = parts(table)
    return np.concatenate([high, high, low], axis=1)


def pair(table):
    return np.stack(parts(table))


def real_basis(positions):
    order = np.arange(HALF + 1)[:, None] * positions[None, :] % WINDOW * UNIT
    return np.concatenate([np.cos(order), np.sin(order)[1:]], axis=0)


def make_tables():
    t = {}
    pixels = np.arange(TILE)
    rows = np.zeros((3, PACK, 8, TILE))
    cols = np.zeros((3, TILE, TILE))
    for d in range(3):
        basis = real_basis(pixels + TILE * (d - 1))
        rows[d, :, :PACK] = basis.reshape(PACK, PACK, TILE)
        for j in range(PACK):
            cols[d, :, REAL * j : REAL * (j + 1)] = basis.T / WINDOW
    t["dft_rows"] = left3(rows.reshape(3 * PACK * 8, TILE))
    t["dft_cols"] = pair(cols.transpose(1, 0, 2).reshape(TILE, 3 * TILE))
    lane_group = np.zeros((PACK, 8, TILE), np.float32)
    for j in range(PACK):
        lane_group[j, :, REAL * j : REAL * (j + 1)] = 1.0

    pick = np.zeros((PACK, BAND, 2 * TILE), np.float32)
    spread = np.zeros((2, TILE, 2, GROUP, 32))
    for row, f in enumerate(FREQ):
        a = abs(f)
        j, i = divmod(a, PACK)
        pick[i, row, REAL * j : REAL * (j + 1)] = 1.0
        if f:
            j, i = divmod(HALF + a, PACK)
            pick[i, row, TILE + REAL * j : TILE + REAL * (j + 1)] = np.sign(f)
    for j in range(PACK):
        for col, g in enumerate(FREQ):
            cos_at = REAL * j + abs(g)
            spread[0, cos_at, 0, :, col] = 1.0
            spread[1, cos_at, 1, :, col] = -1.0
            if g:
                sin_at = REAL * j + HALF + abs(g)
                spread[1, sin_at, 0, :, col] = -np.sign(g)
                spread[0, sin_at, 1, :, col] = -np.sign(g)
    t["pick"] = pick
    t["lane_group"] = lane_group
    t["spread"] = spread.reshape(2 * TILE, 2 * TILE).astype(ml_dtypes.bfloat16)

    flat = np.arange(640)
    rows_of = np.zeros((BAND, 640), np.float32)
    fold = np.zeros((640, GROUP, 32))
    for l in range(BAND * BAND):
        rows_of[l // BAND, l] = 1.0
        fold[l, :, l % BAND] = 1.0
    t["rows_of"] = rows_of[:, : BAND * BAND]
    t["fold"] = fold.reshape(640, TILE)[: BAND * BAND].astype(ml_dtypes.bfloat16)

    angle = FREQ[:, None] * np.arange(GRID)[None, :] % GRID * (2.0 * math.pi / GRID)
    c, s = np.cos(angle), np.sin(angle)
    field_rows = np.block([[c.T, -s.T], [s.T, c.T]])
    t["field_rows"] = left3(field_rows)
    t["field_rows_t"] = left3(field_rows.T)
    field_cols = np.zeros((2, GROUP, 32, 2, GROUP, 64))
    for k in range(GROUP):
        field_cols[0, k, :BAND, 0, k, :GRID] = c
        field_cols[1, k, :BAND, 0, k, :GRID] = -s
        field_cols[0, k, :BAND, 1, k, :GRID] = s
        field_cols[1, k, :BAND, 1, k, :GRID] = c
    field_cols = field_cols.reshape(2 * TILE, 4 * TILE)
    t["field_cols"] = pair(field_cols)
    t["field_cols_t"] = pair(field_cols.T.copy())

    step = WINDOW // GRID
    gap = pixels[:, None] - step * np.arange(GRID)[None, :]
    orders = np.arange(1, GRID // 2)
    inter = (1.0 + 2.0 * np.cos(orders * gap[:, :, None] * UNIT).sum(-1)) / GRID
    inter_wide = np.zeros((TILE, GROUP, 64))
    inter_wide[:, :, :GRID] = inter[:, None, :]
    inter_wide = inter_wide.reshape(TILE, 2 * TILE)
    t["inter_rows"] = left3(inter)
    t["inter_rows_t"] = left3(inter.T)
    t["inter_cols"] = pair(inter_wide.T.copy())
    t["inter_cols_t"] = pair(inter_wide)

    turn = FREQ[:, None] * pixels[None, :] % WINDOW * UNIT
    c, s = np.cos(turn), np.sin(turn)
    last_cols = np.zeros((2, GROUP, 32, 2, TILE))
    last_cols[0, :, :BAND, 0] = c / WINDOW
    last_cols[1, :, :BAND, 0] = -s / WINDOW
    last_cols[0, :, :BAND, 1] = -s / WINDOW
    last_cols[1, :, :BAND, 1] = -c / WINDOW
    t["last_cols"] = pair(last_cols.reshape(2 * TILE, 2 * TILE))
    t["last_rows"] = left3(np.concatenate([c, s], axis=0).T)
    return t


TABLES = make_tables()
NAMES = [
    "dft_rows", "dft_cols", "lane_group", "rows_of", "fold", "pick", "spread", "field_rows", "field_cols",
    "inter_cols", "inter_rows", "inter_rows_t", "inter_cols_t", "field_cols_t", "field_rows_t", "last_cols",
]


def split(x):
    high = x.astype(BF)
    return high, (x - high.astype(F32)).astype(BF)


def dot(a, b):
    return jnp.dot(a, b, preferred_element_type=F32)


def dot3(x, table):
    high, low = split(x)
    return dot(high, table[0]) + dot(low, table[0]) + dot(high, table[1])


def stacked3(x):
    high, low = split(x)
    return jnp.concatenate([high, low, high], axis=0)


def main_kernel(*refs):
    n = len(NAMES)
    mask_hbm, target_hbm, kernels_hbm, cond_ref, dose_ref = refs[:5]
    tables_hbm = refs[5 : 5 + n]
    out_ref = refs[5 + n]
    scratch = refs[6 + n :]
    tab = dict(zip(NAMES, scratch[:n]))
    mask, target, kernels, kk, sent, held, swap, load_sem, send_sem, recv_sem = scratch[n:]

    row, col, core = (lax.axis_index(a) for a in ("row", "col", "cond"))
    n_row, n_col = lax.axis_size("row"), lax.axis_size("col")

    copies = {}
    for i, (name, src, dst) in enumerate(
        [("mask", mask_hbm, mask)]
        + [(m, s, tab[m]) for m, s in zip(NAMES[:3], tables_hbm[:3])]
        + [("kernels", kernels_hbm, kernels)]
        + [(m, s, tab[m]) for m, s in zip(NAMES[3:], tables_hbm[3:])]
        + [("target", target_hbm, target)]
    ):
        copies[name] = pltpu.make_async_copy(src, dst, load_sem.at[i])
        copies[name].start()

    held[...] = jnp.zeros_like(held)
    barrier = pltpu.get_barrier_semaphore()
    count = jnp.int32(1)
    pl.semaphore_signal(barrier, inc=1, device_id=(row, col, 1 - core), device_id_type=MESH)
    there = []
    for dr, dc in OFFSETS:
        ok = (row + dr >= 0) & (row + dr < n_row) & (col + dc >= 0) & (col + dc < n_col)
        there.append(ok)
        count = count + ok.astype(jnp.int32)

        @pl.when(ok)
        def _():
            pl.semaphore_signal(barrier, inc=1, device_id=(row + dr, col + dc, core), device_id_type=MESH)

    for name in ("mask", "dft_rows", "dft_cols", "lane_group"):
        copies[name].wait()
    partial = dot(tab["dft_rows"][...], stacked3(mask[...]))
    blocks = dot3(partial, tab["dft_cols"])
    own = None
    at = 0
    for d in range(3):
        for e in range(3):
            block = None
            for j in range(PACK):
                piece = blocks[8 * (PACK * d + j) : 8 * (PACK * d + j + 1), TILE * e : TILE * (e + 1)]
                piece = piece * tab["lane_group"][j]
                block = piece if block is None else block + piece
            if d == 1 and e == 1:
                own = block
            else:
                sent[at] = block[:PACK]
                at += 1

    pl.semaphore_wait(barrier, count)
    sends = []
    for i, (dr, dc) in enumerate(OFFSETS):
        copy = pltpu.make_async_remote_copy(
            src_ref=sent.at[i],
            dst_ref=held.at[i],
            send_sem=send_sem.at[i],
            recv_sem=recv_sem.at[i],
            device_id=(row - dr, col - dc, core),
            device_id_type=MESH,
        )
        sends.append(copy)

        @pl.when(there[len(OFFSETS) - 1 - i])
        def _(copy=copy):
            copy.start()

    for name in ("kernels", "rows_of", "fold"):
        copies[name].wait()
    lane = lax.broadcasted_iota(jnp.int32, (BAND, TILE), 1) // 32

    def arrange(step, carry):
        c = step // 3
        group = step - 3 * c
        setting = cond_ref[c]
        for part in range(2):
            total = jnp.zeros((BAND, TILE), F32)
            for k in range(GROUP):
                line = kernels[setting, part, pl.ds(group * GROUP + k, 1), :]
                high, low = split(line * tab["rows_of"][...])
                folded = dot(high, tab["fold"][...]) + dot(low, tab["fold"][...])
                total = total + jnp.where(lane == k, folded, 0.0)
            kk[part, step] = total
        return carry

    lax.fori_loop(0, TILES, arrange, 0)
    for name in NAMES[5:] + ["target"]:
        copies[name].wait()
    doses = [dose_ref[cond_ref[c]] for c in range(CONDS)]
    goal = target[...].astype(F32)

    for i in range(len(OFFSETS)):

        @pl.when(there[i])
        def _(i=i):
            sends[i].wait_recv()

    z = own[:PACK]
    for i in range(len(OFFSETS)):
        z = z + held[i]
    chosen = None
    for i in range(PACK):
        line = jnp.concatenate([z[i : i + 1], z[i : i + 1]], axis=1)
        piece = line * tab["pick"][i]
        chosen = piece if chosen is None else chosen + piece
    high, low = split(chosen)
    spectrum = dot(high, tab["spread"][...]) + dot(low, tab["spread"][...])
    s_re, s_im = spectrum[:, :TILE], spectrum[:, TILE:]
    product = []
    for j in range(TILES):
        k_re, k_im = kk[0, j], kk[1, j]
        product.append(jnp.concatenate([k_re * s_re - k_im * s_im, k_re * s_im + k_im * s_re], axis=0))
    along = dot(tab["field_rows"][...], stacked3(jnp.concatenate(product, axis=1)))
    along = jnp.concatenate(
        [
            jnp.concatenate([along[:GRID, TILE * j : TILE * (j + 1)], along[GRID:, TILE * j : TILE * (j + 1)]], axis=1)
            for j in range(TILES)
        ],
        axis=0,
    )
    field = dot3(along, tab["field_cols"])
    square = field * field
    square = square[:, : 2 * TILE] + square[:, 2 * TILE :]
    samples = []
    for c in range(CONDS):
        at = c * (TILES // CONDS) * GRID
        samples.append(square[at : at + GRID] + square[at + GRID : at + 2 * GRID] + square[at + 2 * GRID : at + 3 * GRID])
    inten = dot3(jnp.concatenate(samples, axis=0), tab["inter_cols"])
    inten = jnp.concatenate([inten[:GRID], inten[GRID:]], axis=1)
    inten = dot(tab["inter_rows"][...], stacked3(inten))
    slopes = []
    for c in range(CONDS):
        scale = doses[c] * (STEEP / (KERNELS * BAND * BAND))
        arg = scale * inten[:, TILE * c : TILE * (c + 1)] - STEEP * THRESH
        e = jnp.exp(-jnp.abs(arg))
        inverse = 1.0 / (1.0 + e)
        resist = jnp.where(arg >= 0, inverse, e * inverse)
        slopes.append((resist - goal) * (e * inverse * inverse) * (4.0 * scale))
    back = dot(tab["inter_rows_t"][...], stacked3(jnp.concatenate(slopes, axis=1)))
    back = jnp.concatenate([back[:, :TILE], back[:, TILE:]], axis=0)
    weight = dot3(back, tab["inter_cols_t"])
    pulled = []
    for j in range(TILES):
        at = j // (TILES // CONDS) * GRID
        w = weight[at : at + GRID]
        pulled.append(field[GRID * j : GRID * (j + 1)] * jnp.concatenate([w, w], axis=1))
    pulled = dot3(jnp.concatenate(pulled, axis=0), tab["field_cols_t"])
    pulled = jnp.concatenate(
        [
            jnp.concatenate([pulled[GRID * j : GRID * (j + 1), TILE * p : TILE * (p + 1)] for j in range(TILES)], axis=1)
            for p in range(2)
        ],
        axis=0,
    )
    pulled = dot(tab["field_rows_t"][...], stacked3(pulled))
    d_re = d_im = None
    for j in range(TILES):
        k_re, k_im = kk[0, j], kk[1, j]
        p_re = pulled[:BAND, TILE * j : TILE * (j + 1)]
        p_im = pulled[BAND:, TILE * j : TILE * (j + 1)]
        re, im = k_re * p_re + k_im * p_im, k_re * p_im - k_im * p_re
        d_re, d_im = (re, im) if d_re is None else (d_re + re, d_im + im)
    last = dot3(jnp.concatenate([d_re, d_im], axis=1), tab["last_cols"])
    swap[0, :BAND] = last[:, :TILE]
    swap[0, BAND:] = last[:, TILE:]
    copy = pltpu.make_async_remote_copy(
        src_ref=swap.at[0],
        dst_ref=swap.at[1],
        send_sem=send_sem.at[len(OFFSETS)],
        recv_sem=recv_sem.at[len(OFFSETS)],
        device_id=(row, col, 1 - core),
        device_id_type=MESH,
    )
    copy.start()
    for i in range(len(OFFSETS)):

        @pl.when(there[len(OFFSETS) - 1 - i])
        def _(i=i):
            sends[i].wait_send()

    copy.wait()
    out_ref[...] = swap[0] + swap[1]


def last_kernel(table_ref, sums_ref, out_ref):
    out_ref[...] = dot(table_ref[...], stacked3(sums_ref[...]))


def shards(mask, target, cond_index, kernels, dose):
    any_spec = pl.BlockSpec(memory_space=pl.ANY)
    smem = pl.BlockSpec(memory_space=pltpu.SMEM)
    vmem = pl.BlockSpec(memory_space=pltpu.VMEM)
    tables = [jnp.asarray(TABLES[name]) for name in NAMES]
    sums = pl.pallas_call(
        main_kernel,
        out_shape=jax.ShapeDtypeStruct((2 * BAND, TILE), F32),
        in_specs=[any_spec, any_spec, any_spec, smem, smem] + [any_spec] * len(tables),
        out_specs=vmem,
        scratch_shapes=[pltpu.VMEM(x.shape, x.dtype) for x in tables]
        + [
            pltpu.VMEM(mask.shape, F32),
            pltpu.VMEM(target.shape, jnp.int32),
            pltpu.VMEM(kernels.shape, F32),
            pltpu.VMEM((2, TILES, BAND, TILE), F32),
            pltpu.VMEM((len(OFFSETS), PACK, TILE), F32),
            pltpu.VMEM((len(OFFSETS), PACK, TILE), F32),
            pltpu.VMEM((2, 2 * BAND, TILE), F32),
            pltpu.SemaphoreType.DMA((len(tables) + 3,)),
            pltpu.SemaphoreType.DMA((len(OFFSETS) + 1,)),
            pltpu.SemaphoreType.DMA((len(OFFSETS) + 1,)),
        ],
        compiler_params=pltpu.CompilerParams(
            collective_id=0, has_side_effects=True, vmem_limit_bytes=48 * 1024 * 1024
        ),
        name="spectra_and_gradient",
    )(mask, target, kernels, cond_index, dose, *tables)
    return pl.pallas_call(
        last_kernel,
        out_shape=jax.ShapeDtypeStruct(mask.shape, F32),
        in_specs=[vmem, vmem],
        out_specs=vmem,
        name="to_pixels",
    )(jnp.asarray(TABLES["last_rows"]), sums)


def solution(mesh):
    in_specs = (P("row", "col"), P("row", "col"), P("cond"), P(), P())
    out_specs = P("row", "col")
    return jax.shard_map(shards, mesh=mesh, in_specs=in_specs, out_specs=out_specs, check_vma=False)
```

time: 133 us -> 39.5 us (0.30)
  waiting for transfers between devices: 56.4 us -> 0 us
  Pallas kernels: 0 us -> 23.9 us
  between operations: 20.5 us -> 0.07 us
  starting transfers between devices: 17.2 us -> 0 us
  matrix products: 14.1 us -> 0 us
  other arithmetic: 7.17 us -> 0 us
  local copies, waits for them, and re-layouts: 16.5 us -> 14.7 us
    psum x1 -> x0, waiting for transfers between devices: 46.6 us -> none  [shards(): return lax.psum(local_terms, 'cond')]
    pallas_call x0 -> x2, Pallas kernels: none -> 23.9 us  [the longest x1 22.3 us: shards(): pl.pallas_call(main_kernel, out_shape=jax.ShapeDtypeStruct((2 * BAND, TIL...]
    ppermute x4 -> x0, starting transfers between devices: 17.2 us -> none  [the longest x2 14.6 us: extended(): lax.ppermute(lax.slice_in_dim(block, block.shape[dim] - width, None, axis...]
    dot_general x12 -> x0, matrix products: 14.1 us -> none  [highest(): jnp.dot(left_side, right_side, precision=lax.Precision.HIGHEST, preferred...]
    unnamed x15 -> x43, local copies, waits for them, and re-layouts: 2.4 us -> 14.7 us
    ppermute x4 -> x0, waiting for transfers between devices: 9.71 us -> none  [the longest x2 7.92 us: extended(): lax.ppermute(lax.slice_in_dim(block, 0, width, axis=dim), axis, backward)]
    reshape x10 -> x0, local copies, waits for them, and re-layouts: 6.45 us -> none  [the longest x2 4.94 us: tile_loss(): squared = (fields * fields).reshape(kernel_count, tile_size, 2, tile_size)]
    reduce_sum x4 -> x0, other arithmetic: 4.07 us -> none  [the longest x2 3.94 us: tile_loss(): jnp.sum(squared, axis=(0, 2)) / (kernel_count * band_size * band_size)]
  transfers between devices with their start and end apart: 5 -> 0, of which waited for: 3 -> 0; matrix products, arithmetic and copies ran while one was open for 4% -> 0% of each run, Pallas kernels for 0% -> 0%
where the time goes in v1:
time: 39.5 us; the launch traced here: 38.7 us
  Pallas kernels  23.9 us (61%)
  local copies, waits for them, and re-layouts  14.7 us (37%)
    pallas_call x1, Pallas kernels, shards(): pl.pallas_call(main_kernel, out_shape=jax.ShapeDtypeStruct((2 * BAND, TIL...  22.3 us
    unnamed x43, local copies, waits for them, and re-layouts  14.7 us
    pallas_call x1, Pallas kernels, shards(): pl.pallas_call(last_kernel, out_shape=jax.ShapeDtypeStruct(mask.shape, F3...  1.62 us

profile of v1, /device:TPU:1, one launch (start us, length us, event | category | flops | bytes accessed | tf_op | source)
XLA Modules:
  0.0 38.7 jit_solution(9594802961157536759)
XLA Ops:
  0.0 0.0 copy-start
  0.0 0.0 copy-start.1
  0.0 0.0 copy-start.10
  0.0 0.0 copy-start.20
  0.0 0.0 copy-start.19
  0.0 1.2 %copy.23.refs_2_ = f32[8,2,12,576]{3,2,1,0:T(8,128)S(1)} copy(f32[8,2,12,576]{3,1,2,0:T(2,128)} %param.25) | data formatting | bytes 884736 | tf_op args[3]
  1.2 0.0 copy-done
  1.2 0.1 copy-done.1
  1.3 0.0 copy-done.10
  1.4 0.0 copy-done.20
  1.4 0.0 copy-done.19
  1.4 0.0 copy-start.2
  1.4 0.9 %copy-done.2 = bf16[2,256,256]{2,1,0:T(8,128)(2,1)S(1)} copy-done((bf16[2,256,256]{2,1,0:T(8,128)(2,1)S(1)}, bf16[2,256,256]{2,1,0:T(8,128)(2,1)}, u32[]{:S(2)}) %copy-start.2) | copy-done | bytes 262168
  2.3 0.0 copy-start.3
  2.3 0.9 %copy-done.3 = bf16[2,128,384]{2,1,0:T(8,128)(2,1)S(1)} copy-done((bf16[2,128,384]{2,1,0:T(8,128)(2,1)S(1)}, bf16[2,128,384]{2,1,0:T(8,128)(2,1)}, u32[]{:S(2)}) %copy-start.3) | copy-done | bytes 196632
  3.2 0.0 copy-start.4
  3.2 0.9 %copy-done.4 = bf16[576,128]{1,0:T(8,128)(2,1)S(1)} copy-done((bf16[576,128]{1,0:T(8,128)(2,1)S(1)}, bf16[576,128]{1,0:T(8,128)(2,1)}, u32[]{:S(2)}) %copy-start.4) | copy-done | bytes 147480
  4.1 0.0 copy-start.5
  4.2 0.9 %copy-done.5 = bf16[2,128,256]{2,1,0:T(8,128)(2,1)S(1)} copy-done((bf16[2,128,256]{2,1,0:T(8,128)(2,1)S(1)}, bf16[2,128,256]{2,1,0:T(8,128)(2,1)}, u32[]{:S(2)}) %copy-start.5) | copy-done | bytes 131096
  5.1 0.0 copy-start.6
  5.1 0.9 %copy-done.6 = bf16[2,256,128]{2,1,0:T(8,128)(2,1)S(1)} copy-done((bf16[2,256,128]{2,1,0:T(8,128)(2,1)S(1)}, bf16[2,256,128]{2,1,0:T(8,128)(2,1)}, u32[]{:S(2)}) %copy-start.6) | copy-done | bytes 131096
  6.0 0.0 copy-start.7
  6.0 0.9 %copy-done.7 = bf16[256,256]{1,0:T(8,128)(2,1)S(1)} copy-done((bf16[256,256]{1,0:T(8,128)(2,1)S(1)}, bf16[256,256]{1,0:T(8,128)(2,1)}, u32[]{:S(2)}) %copy-start.7) | copy-done | bytes 131096
  6.9 0.0 copy-start.8
  6.9 0.9 %copy-done.8 = f32[5,24,256]{2,1,0:T(8,128)S(1)} copy-done((f32[5,24,256]{2,1,0:T(8,128)S(1)}, f32[5,24,256]{2,1,0:T(8,128)}, u32[]{:S(2)}) %copy-start.8) | copy-done | bytes 122904
  7.8 0.0 copy-start.11
  7.8 0.8 %copy-done.11 = f32[128,128]{1,0:T(8,128)S(1)} copy-done((f32[128,128]{1,0:T(8,128)S(1)}, f32[128,128]{1,0:T(8,128)}, u32[]{:S(2)}) %copy-start.11) | copy-done | bytes 65560
  8.6 0.0 copy-start.12
  8.6 0.8 %copy-done.12 = s32[128,128]{1,0:T(8,128)S(1)} copy-done((s32[128,128]{1,0:T(8,128)S(1)}, s32[128,128]{1,0:T(8,128)}, u32[]{:S(2)}) %copy-start.12) | copy-done | bytes 65560
  9.4 0.0 copy-start.13
  9.4 0.8 %copy-done.13 = bf16[128,144]{1,0:T(8,128)(2,1)S(1)} copy-done((bf16[128,144]{1,0:T(8,128)(2,1)S(1)}, bf16[128,144]{1,0:T(8,128)(2,1)}, u32[]{:S(2)}) %copy-start.13) | copy-done | bytes 36888
  10.3 0.0 copy-start.14
  10.3 0.8 %copy-done.14 = f32[24,576]{1,0:T(8,128)S(1)} copy-done((f32[24,576]{1,0:T(8,128)S(1)}, f32[24,576]{1,0:T(8,128)}, u32[]{:S(2)}) %copy-start.14) | copy-done | bytes 55320
  11.1 0.0 copy-start.15
  11.1 0.8 %copy-done.15 = bf16[96,144]{1,0:T(8,128)(2,1)S(1)} copy-done((bf16[96,144]{1,0:T(8,128)(2,1)S(1)}, bf16[96,144]{1,0:T(8,128)(2,1)}, u32[]{:S(2)}) %copy-start.15) | copy-done | bytes 27672
  11.9 0.0 copy-start.16
  11.9 0.8 %copy-done.16 = bf16[48,288]{1,0:T(8,128)(2,1)S(1)} copy-done((bf16[48,288]{1,0:T(8,128)(2,1)S(1)}, bf16[48,288]{1,0:T(8,128)(2,1)}, u32[]{:S(2)}) %copy-start.16) | copy-done | bytes 27672
  12.7 0.0 copy-start.17
  12.7 0.8 %copy-done.17 = bf16[48,384]{1,0:T(8,128)(2,1)S(1)} copy-done((bf16[48,384]{1,0:T(8,128)(2,1)S(1)}, bf16[48,384]{1,0:T(8,128)(2,1)}, u32[]{:S(2)}) %copy-start.17) | copy-done | bytes 36888
  13.4 0.0 copy-start.18
  13.5 0.7 %copy-done.18 = f32[5,8,128]{2,1,0:T(8,128)S(1)} copy-done((f32[5,8,128]{2,1,0:T(8,128)S(1)}, f32[5,8,128]{2,1,0:T(8,128)}, u32[]{:S(2)}) %copy-start.18) | copy-done | bytes 20504
  14.2 22.3 %spectra_and_gradient.1.sums_ref = f32[48,128]{1,0:T(8,128)S(1)} custom-call(f32[128,128]{1,0:T(8,128)S(1)} %copy-done.11, s32[128,128]{1,0:T(8,128)S(1)} %copy-done.12, f32[8,2,12,576]{3,2,1,0:T(8,128)S(1)} %copy.23.refs_2_, s32[2]{0:T(128)S(1)} %copy-done.19, f32[8]{0:T(128)S(1)} %copy-done.20, bf16[120,384]{1,0:T(8,128)(2,1)S(1)} %copy-done.10, ...), custom_call_target="tpu_custom_call" | custom-call | tf_op jit(solution)/shard_map/spectra_and_gradient/pallas_call | solution.py:367
  36.5 0.0 copy-start.9
  36.5 0.6 %copy-done.9 = f32[48,128]{1,0:T(8,128)} copy-done((f32[48,128]{1,0:T(8,128)}, f32[48,128]{1,0:T(8,128)S(1)}, u32[]{:S(2)}) %copy-start.9) | copy-done | bytes 24600
  37.1 1.6 %to_pixels.1 = f32[128,128]{1,0:T(8,128)} custom-call(bf16[128,144]{1,0:T(8,128)(2,1)} %constant.50.clone.table_ref, f32[48,128]{1,0:T(8,128)} %copy-done.9), custom_call_target="tpu_custom_call" | custom-call | tf_op jit(solution)/shard_map/to_pixels/pallas_call | solution.py:390
Async XLA Ops:
  0.0 1.2 %copy-start = (bf16[2,512,256]{2,1,0:T(8,128)(2,1)S(1)}, bf16[2,512,256]{2,1,0:T(8,128)(2,1)}, u32[]{:S(2)}) copy-start(bf16[2,512,256]{2,1,0:T(8,128)(2,1)} %constant.47.clone.refs_18_) | copy-start | bytes 1572868
  0.0 1.3 %copy-start.1 = (bf16[2,256,512]{2,1,0:T(8,128)(2,1)S(1)}, bf16[2,256,512]{2,1,0:T(8,128)(2,1)}, u32[]{:S(2)}) copy-start(bf16[2,256,512]{2,1,0:T(8,128)(2,1)} %constant.42.clone.refs_13_) | copy-start | bytes 1572868
  0.0 1.3 %copy-start.10 = (bf16[120,384]{1,0:T(8,128)(2,1)S(1)}, bf16[120,384]{1,0:T(8,128)(2,1)}, u32[]{:S(2)}) copy-start(bf16[120,384]{1,0:T(8,128)(2,1)} %constant.34.clone.refs_5_) | copy-start | bytes 276484
  0.0 1.3 %copy-start.20 = (f32[8]{0:T(128)S(1)}, f32[8]{0:T(128)}, u32[]{:S(2)}) copy-start(f32[8]{0:T(128)} %refs_4_.1) | copy-start | bytes 100
  0.0 1.3 %copy-start.19 = (s32[2]{0:T(128)S(1)}, s32[2]{0:T(128)}, u32[]{:S(2)}) copy-start(s32[2]{0:T(128)} %refs_3_.1) | copy-start | bytes 28
  1.4 1.0 %copy-start.2 = (bf16[2,256,256]{2,1,0:T(8,128)(2,1)S(1)}, bf16[2,256,256]{2,1,0:T(8,128)(2,1)}, u32[]{:S(2)}) copy-start(bf16[2,256,256]{2,1,0:T(8,128)(2,1)} %constant.49.clone.refs_20_) | copy-start | bytes 786436
  2.3 0.9 %copy-start.3 = (bf16[2,128,384]{2,1,0:T(8,128)(2,1)S(1)}, bf16[2,128,384]{2,1,0:T(8,128)(2,1)}, u32[]{:S(2)}) copy-start(bf16[2,128,384]{2,1,0:T(8,128)(2,1)} %constant.35.clone.refs_6_) | copy-start | bytes 589828
  3.2 0.9 %copy-start.4 = (bf16[576,128]{1,0:T(8,128)(2,1)S(1)}, bf16[576,128]{1,0:T(8,128)(2,1)}, u32[]{:S(2)}) copy-start(bf16[576,128]{1,0:T(8,128)(2,1)} %constant.38.clone.refs_9_) | copy-start | bytes 442372
  4.1 0.9 %copy-start.5 = (bf16[2,128,256]{2,1,0:T(8,128)(2,1)S(1)}, bf16[2,128,256]{2,1,0:T(8,128)(2,1)}, u32[]{:S(2)}) copy-start(bf16[2,128,256]{2,1,0:T(8,128)(2,1)} %constant.46.clone.refs_17_) | copy-start | bytes 393220
  5.1 0.9 %copy-start.6 = (bf16[2,256,128]{2,1,0:T(8,128)(2,1)S(1)}, bf16[2,256,128]{2,1,0:T(8,128)(2,1)}, u32[]{:S(2)}) copy-start(bf16[2,256,128]{2,1,0:T(8,128)(2,1)} %constant.43.clone.refs_14_) | copy-start | bytes 393220
  6.0 0.9 %copy-start.7 = (bf16[256,256]{1,0:T(8,128)(2,1)S(1)}, bf16[256,256]{1,0:T(8,128)(2,1)}, u32[]{:S(2)}) copy-start(bf16[256,256]{1,0:T(8,128)(2,1)} %constant.40.clone.refs_11_) | copy-start | bytes 393220
  6.9 0.9 %copy-start.8 = (f32[5,24,256]{2,1,0:T(8,128)S(1)}, f32[5,24,256]{2,1,0:T(8,128)}, u32[]{:S(2)}) copy-start(f32[5,24,256]{2,1,0:T(8,128)} %constant.39.clone.refs_10_) | copy-start | bytes 368644
  7.8 0.8 %copy-start.11 = (f32[128,128]{1,0:T(8,128)S(1)}, f32[128,128]{1,0:T(8,128)}, u32[]{:S(2)}) copy-start(f32[128,128]{1,0:T(8,128)} %refs_0_.1) | copy-start | bytes 196612
  8.6 0.8 %copy-start.12 = (s32[128,128]{1,0:T(8,128)S(1)}, s32[128,128]{1,0:T(8,128)}, u32[]{:S(2)}) copy-start(s32[128,128]{1,0:T(8,128)} %refs_1_.1) | copy-start | bytes 196612
  9.4 0.8 %copy-start.13 = (bf16[128,144]{1,0:T(8,128)(2,1)S(1)}, bf16[128,144]{1,0:T(8,128)(2,1)}, u32[]{:S(2)}) copy-start(bf16[128,144]{1,0:T(8,128)(2,1)} %constant.44.clone.refs_15_) | copy-start | bytes 110596
  10.3 0.8 %copy-start.14 = (f32[24,576]{1,0:T(8,128)S(1)}, f32[24,576]{1,0:T(8,128)}, u32[]{:S(2)}) copy-start(f32[24,576]{1,0:T(8,128)} %constant.37.clone.refs_8_) | copy-start | bytes 165892
  11.1 0.8 %copy-start.15 = (bf16[96,144]{1,0:T(8,128)(2,1)S(1)}, bf16[96,144]{1,0:T(8,128)(2,1)}, u32[]{:S(2)}) copy-start(bf16[96,144]{1,0:T(8,128)(2,1)} %constant.41.clone.refs_12_) | copy-start | bytes 82948
  11.9 0.8 %copy-start.16 = (bf16[48,288]{1,0:T(8,128)(2,1)S(1)}, bf16[48,288]{1,0:T(8,128)(2,1)}, u32[]{:S(2)}) copy-start(bf16[48,288]{1,0:T(8,128)(2,1)} %constant.48.clone.refs_19_) | copy-start | bytes 82948
  12.7 0.8 %copy-start.17 = (bf16[48,384]{1,0:T(8,128)(2,1)S(1)}, bf16[48,384]{1,0:T(8,128)(2,1)}, u32[]{:S(2)}) copy-start(bf16[48,384]{1,0:T(8,128)(2,1)} %constant.45.clone.refs_16_) | copy-start | bytes 110596
  13.4 0.7 %copy-start.18 = (f32[5,8,128]{2,1,0:T(8,128)S(1)}, f32[5,8,128]{2,1,0:T(8,128)}, u32[]{:S(2)}) copy-start(f32[5,8,128]{2,1,0:T(8,128)} %constant.36.clone.refs_7_) | copy-start | bytes 61444
  36.5 0.6 %copy-start.9 = (f32[48,128]{1,0:T(8,128)}, f32[48,128]{1,0:T(8,128)S(1)}, u32[]{:S(2)}) copy-start(f32[48,128]{1,0:T(8,128)S(1)} %spectra_and_gradient.1.sums_ref) | copy-start | bytes 73732

commit v2 on v1

--- a/solution.py
+++ b/solution.py
@@ -167,12 +167,12 @@
 
 def main_kernel(*refs):
     n = len(NAMES)
-    mask_hbm, target_hbm, kernels_hbm, cond_ref, dose_ref = refs[:5]
+    mask_hbm, target_hbm, kernels_hbm, cond_hbm, dose_hbm = refs[:5]
     tables_hbm = refs[5 : 5 + n]
     out_ref = refs[5 + n]
     scratch = refs[6 + n :]
     tab = dict(zip(NAMES, scratch[:n]))
-    mask, target, kernels, kk, sent, held, swap, load_sem, send_sem, recv_sem = scratch[n:]
+    mask, target, kernels, cond_ref, dose_ref, kk, sent, held, swap, load_sem, send_sem, recv_sem = scratch[n:]
 
     row, col, core = (lax.axis_index(a) for a in ("row", "col", "cond"))
     n_row, n_col = lax.axis_size("row"), lax.axis_size("col")
@@ -181,7 +181,7 @@
     for i, (name, src, dst) in enumerate(
         [("mask", mask_hbm, mask)]
         + [(m, s, tab[m]) for m, s in zip(NAMES[:3], tables_hbm[:3])]
-        + [("kernels", kernels_hbm, kernels)]
+        + [("kernels", kernels_hbm, kernels), ("cond", cond_hbm, cond_ref), ("dose", dose_hbm, dose_ref)]
         + [(m, s, tab[m]) for m, s in zip(NAMES[3:], tables_hbm[3:])]
         + [("target", target_hbm, target)]
     ):
@@ -238,7 +238,7 @@
         def _(copy=copy):
             copy.start()
 
-    for name in ("kernels", "rows_of", "fold"):
+    for name in ("kernels", "cond", "dose", "rows_of", "fold"):
         copies[name].wait()
     lane = lax.broadcasted_iota(jnp.int32, (BAND, TILE), 1) // 32
 
@@ -249,7 +249,7 @@
         for part in range(2):
             total = jnp.zeros((BAND, TILE), F32)
             for k in range(GROUP):
-                line = kernels[setting, part, pl.ds(group * GROUP + k, 1), :]
+                line = kernels[setting, group * GROUP + k, part : part + 1, :]
                 high, low = split(line * tab["rows_of"][...])
                 folded = dot(high, tab["fold"][...]) + dot(low, tab["fold"][...])
                 total = total + jnp.where(lane == k, folded, 0.0)
@@ -361,32 +361,34 @@
 
 def shards(mask, target, cond_index, kernels, dose):
     any_spec = pl.BlockSpec(memory_space=pl.ANY)
-    smem = pl.BlockSpec(memory_space=pltpu.SMEM)
     vmem = pl.BlockSpec(memory_space=pltpu.VMEM)
     tables = [jnp.asarray(TABLES[name]) for name in NAMES]
+    by_kernel = jnp.transpose(kernels, (0, 2, 1, 3))
     sums = pl.pallas_call(
         main_kernel,
         out_shape=jax.ShapeDtypeStruct((2 * BAND, TILE), F32),
-        in_specs=[any_spec, any_spec, any_spec, smem, smem] + [any_spec] * len(tables),
+        in_specs=[any_spec] * (5 + len(tables)),
         out_specs=vmem,
         scratch_shapes=[pltpu.VMEM(x.shape, x.dtype) for x in tables]
         + [
             pltpu.VMEM(mask.shape, F32),
             pltpu.VMEM(target.shape, jnp.int32),
-            pltpu.VMEM(kernels.shape, F32),
+            pltpu.VMEM(by_kernel.shape, F32),
+            pltpu.SMEM(cond_index.shape, jnp.int32),
+            pltpu.SMEM(dose.shape, F32),
             pltpu.VMEM((2, TILES, BAND, TILE), F32),
             pltpu.VMEM((len(OFFSETS), PACK, TILE), F32),
             pltpu.VMEM((len(OFFSETS), PACK, TILE), F32),
             pltpu.VMEM((2, 2 * BAND, TILE), F32),
-            pltpu.SemaphoreType.DMA((len(tables) + 3,)),
+            pltpu.SemaphoreType.DMA((len(tables) + 5,)),
             pltpu.SemaphoreType.DMA((len(OFFSETS) + 1,)),
             pltpu.SemaphoreType.DMA((len(OFFSETS) + 1,)),
         ],
         compiler_params=pltpu.CompilerParams(
-            collective_id=0, has_side_effects=True, vmem_limit_bytes=48 * 1024 * 1024
+            collective_id=0, has_side_effects=True, vmem_limit_bytes=63 * 1024 * 1024
         ),
         name="spectra_and_gradient",
-    )(mask, target, kernels, cond_index, dose, *tables)
+    )(mask, target, by_kernel, cond_index, dose, *tables)
     return pl.pallas_call(
         last_kernel,
         out_shape=jax.ShapeDtypeStruct(mask.shape, F32),

time: 39.5 us -> 22 us (0.56); the launches traced: 38.7 us -> 21.9 us
  local copies, waits for them, and re-layouts: 14.7 us -> 0 us
  Pallas kernels: 23.9 us -> 21.9 us
    unnamed x43 -> x0, local copies, waits for them, and re-layouts: 14.7 us -> none
    pallas_call x1, Pallas kernels: 22.3 us -> 20.2 us  [shards(): pl.pallas_call(main_kernel, out_shape=jax.ShapeDtypeStruct((2 * BAND, TIL...]
where the time goes in v2:
time: 22 us; the launch traced here: 21.9 us
  Pallas kernels  21.9 us (100%)
    pallas_call x1, Pallas kernels, shards(): pl.pallas_call(main_kernel, out_shape=jax.ShapeDtypeStruct((2 * BAND, TIL...  20.2 us
    pallas_call x1, Pallas kernels, shards(): pl.pallas_call(last_kernel, out_shape=jax.ShapeDtypeStruct(mask.shape, F3...  1.63 us

profile of v2, /device:TPU:1, one launch (start us, length us, event | category | flops | bytes accessed | tf_op | source)
XLA Modules:
  0.0 21.9 jit_solution(10183471044030324276)
XLA Ops:
  0.0 20.2 %spectra_and_gradient.1.sums_ref = f32[48,128]{1,0:T(8,128)} custom-call(f32[128,128]{1,0:T(8,128)} %refs_0_.1, s32[128,128]{1,0:T(8,128)} %refs_1_.1, f32[8,12,2,576]{3,2,1,0:T(2,128)} %bitcast.1, s32[2]{0:T(128)} %refs_3_.1, f32[8]{0:T(128)} %refs_4_.1, bf16[120,384]{1,0:T(8,128)(2,1)} %constant.34.clone.refs_5_, ...), custom_call_target="tpu_custom_call" | custom-call | tf_op jit(solution)/shard_map/spectra_and_gradient/pallas_call | solution.py:367
  20.2 1.6 %to_pixels.1 = f32[128,128]{1,0:T(8,128)} custom-call(bf16[128,144]{1,0:T(8,128)(2,1)} %constant.50.clone.table_ref, f32[48,128]{1,0:T(8,128)} %spectra_and_gradient.1.sums_ref), custom_call_target="tpu_custom_call" | custom-call | tf_op jit(solution)/shard_map/to_pixels/pallas_call | solution.py:392

commit v3 on v2

--- a/solution.py
+++ b/solution.py
@@ -28,7 +28,8 @@
 TILES = CONDS * KERNELS // GROUP
 STEEP = 4.0
 THRESH = 0.6
-OFFSETS = [(-1, -1), (-1, 0), (-1, 1), (0, -1), (0, 1), (1, -1), (1, 0), (1, 1)]
+OFFSETS = [(-1, -1), (-1, 1), (0, -1), (-1, 0), (1, 0), (0, 1), (1, -1), (1, 1)]
+ORDER = [(0, 6, 2), (1, 7, 5), (3, 4)]
 FREQ = np.arange(BAND) - HALF
 UNIT = 2.0 * math.pi / WINDOW
 
@@ -65,9 +66,6 @@
             cols[d, :, REAL * j : REAL * (j + 1)] = basis.T / WINDOW
     t["dft_rows"] = left3(rows.reshape(3 * PACK * 8, TILE))
     t["dft_cols"] = pair(cols.transpose(1, 0, 2).reshape(TILE, 3 * TILE))
-    lane_group = np.zeros((PACK, 8, TILE), np.float32)
-    for j in range(PACK):
-        lane_group[j, :, REAL * j : REAL * (j + 1)] = 1.0
 
     pick = np.zeros((PACK, BAND, 2 * TILE), np.float32)
     spread = np.zeros((2, TILE, 2, GROUP, 32))
@@ -88,17 +86,15 @@
                 spread[1, sin_at, 0, :, col] = -np.sign(g)
                 spread[0, sin_at, 1, :, col] = -np.sign(g)
     t["pick"] = pick
-    t["lane_group"] = lane_group
     t["spread"] = spread.reshape(2 * TILE, 2 * TILE).astype(ml_dtypes.bfloat16)
 
-    flat = np.arange(640)
-    rows_of = np.zeros((BAND, 640), np.float32)
-    fold = np.zeros((640, GROUP, 32))
+    rows_of = np.zeros((BAND, BAND * BAND), np.float32)
+    fold = np.zeros((BAND * BAND, GROUP, 32))
     for l in range(BAND * BAND):
         rows_of[l // BAND, l] = 1.0
         fold[l, :, l % BAND] = 1.0
-    t["rows_of"] = rows_of[:, : BAND * BAND]
-    t["fold"] = fold.reshape(640, TILE)[: BAND * BAND].astype(ml_dtypes.bfloat16)
+    t["rows_of"] = rows_of
+    t["fold"] = fold.reshape(BAND * BAND, TILE).astype(ml_dtypes.bfloat16)
 
     angle = FREQ[:, None] * np.arange(GRID)[None, :] % GRID * (2.0 * math.pi / GRID)
     c, s = np.cos(angle), np.sin(angle)
@@ -141,9 +137,12 @@
 
 TABLES = make_tables()
 NAMES = [
-    "dft_rows", "dft_cols", "lane_group", "rows_of", "fold", "pick", "spread", "field_rows", "field_cols",
+    "dft_rows", "dft_cols", "rows_of", "fold", "pick", "spread", "field_rows", "field_cols",
     "inter_cols", "inter_rows", "inter_rows_t", "inter_cols_t", "field_cols_t", "field_rows_t", "last_cols",
+    "last_rows",
 ]
+
+LOADS = ("kernels", "cond", "dose", "rows_of", "fold")
 
 
 def split(x):
@@ -169,77 +168,84 @@
     n = len(NAMES)
     mask_hbm, target_hbm, kernels_hbm, cond_hbm, dose_hbm = refs[:5]
     tables_hbm = refs[5 : 5 + n]
-    out_ref = refs[5 + n]
-    scratch = refs[6 + n :]
-    tab = dict(zip(NAMES, scratch[:n]))
-    mask, target, kernels, cond_ref, dose_ref, kk, sent, held, swap, load_sem, send_sem, recv_sem = scratch[n:]
+    table_ref, out_ref = refs[5 + n : 7 + n]
+    scratch = refs[7 + n :]
+    tab = dict(zip(NAMES, list(scratch[: n - 1]) + [table_ref]))
+    mask, target, kernels, cond_ref, dose_ref, kk, sent, held, swap, load_sem, send_sem, recv_sem = scratch[n - 1 :]
 
     row, col, core = (lax.axis_index(a) for a in ("row", "col", "cond"))
     n_row, n_col = lax.axis_size("row"), lax.axis_size("col")
 
     copies = {}
-    for i, (name, src, dst) in enumerate(
-        [("mask", mask_hbm, mask)]
-        + [(m, s, tab[m]) for m, s in zip(NAMES[:3], tables_hbm[:3])]
-        + [("kernels", kernels_hbm, kernels), ("cond", cond_hbm, cond_ref), ("dose", dose_hbm, dose_ref)]
-        + [(m, s, tab[m]) for m, s in zip(NAMES[3:], tables_hbm[3:])]
+    first = [("mask", mask_hbm, mask)] + [(m, s, tab[m]) for m, s in zip(NAMES[:2], tables_hbm[:2])]
+    later = (
+        [("kernels", kernels_hbm, kernels), ("cond", cond_hbm, cond_ref), ("dose", dose_hbm, dose_ref)]
+        + [(m, s, tab[m]) for m, s in zip(NAMES[2:], tables_hbm[2:])]
         + [("target", target_hbm, target)]
-    ):
+    )
+    for i, (name, src, dst) in enumerate(first + later):
         copies[name] = pltpu.make_async_copy(src, dst, load_sem.at[i])
+    for name, _, _ in first:
         copies[name].start()
 
     held[...] = jnp.zeros_like(held)
     barrier = pltpu.get_barrier_semaphore()
-    count = jnp.int32(1)
     pl.semaphore_signal(barrier, inc=1, device_id=(row, col, 1 - core), device_id_type=MESH)
     there = []
+    count = jnp.int32(1)
     for dr, dc in OFFSETS:
         ok = (row + dr >= 0) & (row + dr < n_row) & (col + dc >= 0) & (col + dc < n_col)
+        sender = 0 if dc == 0 else 1
         there.append(ok)
-        count = count + ok.astype(jnp.int32)
+        count = count + jnp.where(ok & (core == sender), 2, 0)
 
         @pl.when(ok)
         def _():
-            pl.semaphore_signal(barrier, inc=1, device_id=(row + dr, col + dc, core), device_id_type=MESH)
-
-    for name in ("mask", "dft_rows", "dft_cols", "lane_group"):
+            pl.semaphore_signal(barrier, inc=1, device_id=(row + dr, col + dc, sender), device_id_type=MESH)
+
+    for name in ("mask", "dft_rows", "dft_cols"):
         copies[name].wait()
+    lanes = lax.broadcasted_iota(jnp.int32, (8, TILE), 1)
     partial = dot(tab["dft_rows"][...], stacked3(mask[...]))
-    blocks = dot3(partial, tab["dft_cols"])
-    own = None
-    at = 0
-    for d in range(3):
-        for e in range(3):
+    partial = split(partial)
+
+    def blocks_of(e):
+        table = [tab["dft_cols"][p, :, TILE * e : TILE * (e + 1)] for p in range(2)]
+        products = dot(partial[0], table[0]) + dot(partial[1], table[0]) + dot(partial[0], table[1])
+        own = None
+        for d in range(3):
             block = None
             for j in range(PACK):
-                piece = blocks[8 * (PACK * d + j) : 8 * (PACK * d + j + 1), TILE * e : TILE * (e + 1)]
-                piece = piece * tab["lane_group"][j]
-                block = piece if block is None else block + piece
+                piece = products[8 * (PACK * d + j) : 8 * (PACK * d + j + 1)]
+                block = piece if block is None else jnp.where(lanes < REAL * j, block, piece)
             if d == 1 and e == 1:
                 own = block
             else:
-                sent[at] = block[:PACK]
-                at += 1
-
-    pl.semaphore_wait(barrier, count)
-    sends = []
-    for i, (dr, dc) in enumerate(OFFSETS):
-        copy = pltpu.make_async_remote_copy(
-            src_ref=sent.at[i],
-            dst_ref=held.at[i],
-            send_sem=send_sem.at[i],
-            recv_sem=recv_sem.at[i],
-            device_id=(row - dr, col - dc, core),
-            device_id_type=MESH,
-        )
-        sends.append(copy)
-
-        @pl.when(there[len(OFFSETS) - 1 - i])
-        def _(copy=copy):
-            copy.start()
-
-    for name in ("kernels", "cond", "dose", "rows_of", "fold"):
-        copies[name].wait()
+                sent[OFFSETS.index((d - 1, e - 1))] = block[:PACK]
+        return own
+
+    sends = {}
+
+    def send(order):
+        for i in order:
+            dr, dc = OFFSETS[i]
+            for target in range(2):
+                sends[i, target] = pltpu.make_async_remote_copy(
+                    src_ref=sent.at[i],
+                    dst_ref=held.at[i],
+                    send_sem=send_sem.at[2 * i + target],
+                    recv_sem=recv_sem.at[i],
+                    device_id=(row - dr, col - dc, target),
+                    device_id_type=MESH,
+                )
+
+                @pl.when(there[len(OFFSETS) - 1 - i] & (core == (0 if dc == 0 else 1)))
+                def _():
+                    sends[i, target].start()
+
+    blocks_of(0)
+    ahead = jnp.where(lax.rem(col, 2) == 0, TILES, 0)
+
     lane = lax.broadcasted_iota(jnp.int32, (BAND, TILE), 1) // 32
 
     def arrange(step, carry):
@@ -256,8 +262,30 @@
             kk[part, step] = total
         return carry
 
-    lax.fori_loop(0, TILES, arrange, 0)
-    for name in NAMES[5:] + ["target"]:
+    @pl.when(ahead > 0)
+    def _():
+        for name, _, _ in later:
+            copies[name].start()
+        for name in LOADS:
+            copies[name].wait()
+        lax.fori_loop(0, TILES, arrange, 0)
+
+    pl.semaphore_wait(barrier, count)
+    send(ORDER[0])
+    blocks_of(2)
+    send(ORDER[1])
+    own = blocks_of(1)
+    send(ORDER[2])
+
+    @pl.when(ahead == 0)
+    def _():
+        for name, _, _ in later:
+            copies[name].start()
+        for name in LOADS:
+            copies[name].wait()
+        lax.fori_loop(0, TILES, arrange, 0)
+
+    for name in NAMES[4:] + ["target"]:
         copies[name].wait()
     doses = [dose_ref[cond_ref[c]] for c in range(CONDS)]
     goal = target[...].astype(F32)
@@ -266,7 +294,7 @@
 
         @pl.when(there[i])
         def _(i=i):
-            sends[i].wait_recv()
+            sends[i, 0].wait_recv()
 
     z = own[:PACK]
     for i in range(len(OFFSETS)):
@@ -339,24 +367,25 @@
     copy = pltpu.make_async_remote_copy(
         src_ref=swap.at[0],
         dst_ref=swap.at[1],
-        send_sem=send_sem.at[len(OFFSETS)],
+        send_sem=send_sem.at[2 * len(OFFSETS)],
         recv_sem=recv_sem.at[len(OFFSETS)],
         device_id=(row, col, 1 - core),
         device_id_type=MESH,
     )
     copy.start()
-    for i in range(len(OFFSETS)):
-
-        @pl.when(there[len(OFFSETS) - 1 - i])
+    for i, (dr, dc) in enumerate(OFFSETS):
+
+        @pl.when(there[len(OFFSETS) - 1 - i] & (core == (0 if dc == 0 else 1)))
         def _(i=i):
-            sends[i].wait_send()
+            for target in range(2):
+                sends[i, target].wait_send()
 
     copy.wait()
-    out_ref[...] = swap[0] + swap[1]
+    out_ref[...] = stacked3(swap[0] + swap[1])
 
 
 def last_kernel(table_ref, sums_ref, out_ref):
-    out_ref[...] = dot(table_ref[...], stacked3(sums_ref[...]))
+    out_ref[...] = dot(table_ref[...], sums_ref[...])
 
 
 def shards(mask, target, cond_index, kernels, dose):
@@ -364,12 +393,12 @@
     vmem = pl.BlockSpec(memory_space=pltpu.VMEM)
     tables = [jnp.asarray(TABLES[name]) for name in NAMES]
     by_kernel = jnp.transpose(kernels, (0, 2, 1, 3))
-    sums = pl.pallas_call(
+    handed = pl.pallas_call(
         main_kernel,
-        out_shape=jax.ShapeDtypeStruct((2 * BAND, TILE), F32),
+        out_shape=[pltpu.VMEM(tables[-1].shape, BF), pltpu.VMEM((6 * BAND, TILE), BF)],
         in_specs=[any_spec] * (5 + len(tables)),
-        out_specs=vmem,
-        scratch_shapes=[pltpu.VMEM(x.shape, x.dtype) for x in tables]
+        out_specs=[vmem, vmem],
+        scratch_shapes=[pltpu.VMEM(x.shape, x.dtype) for x in tables[:-1]]
         + [
             pltpu.VMEM(mask.shape, F32),
             pltpu.VMEM(target.shape, jnp.int32),
@@ -381,7 +410,7 @@
             pltpu.VMEM((len(OFFSETS), PACK, TILE), F32),
             pltpu.VMEM((2, 2 * BAND, TILE), F32),
             pltpu.SemaphoreType.DMA((len(tables) + 5,)),
-            pltpu.SemaphoreType.DMA((len(OFFSETS) + 1,)),
+            pltpu.SemaphoreType.DMA((2 * len(OFFSETS) + 1,)),
             pltpu.SemaphoreType.DMA((len(OFFSETS) + 1,)),
         ],
         compiler_params=pltpu.CompilerParams(
@@ -395,7 +424,7 @@
         in_specs=[vmem, vmem],
         out_specs=vmem,
         name="to_pixels",
-    )(jnp.asarray(TABLES["last_rows"]), sums)
+    )(*[pltpu.with_memory_space_constraint(x, pltpu.VMEM) for x in handed])
 
 
 def solution(mesh):

time: 22 us -> 20.2 us (0.918)
  Pallas kernels: 21.9 us -> 20.1 us
    pallas_call x1, Pallas kernels: 20.2 us -> 19.3 us  [shards(): pl.pallas_call(main_kernel, out_shape=[pltpu.VMEM(tables[-1].shape, BF),...]
    pallas_call x1, Pallas kernels: 1.63 us -> 0.78 us  [shards(): pl.pallas_call(last_kernel, out_shape=jax.ShapeDtypeStruct(mask.shape, F3...]
where the time goes in v3:
time: 20.2 us; the launch traced here: 20.1 us
  Pallas kernels  20.1 us (100%)
    pallas_call x1, Pallas kernels, shards(): pl.pallas_call(main_kernel, out_shape=[pltpu.VMEM(tables[-1].shape, BF),...  19.3 us
    pallas_call x1, Pallas kernels, shards(): pl.pallas_call(last_kernel, out_shape=jax.ShapeDtypeStruct(mask.shape, F3...  0.78 us

profile of v3, /device:TPU:1, one launch (start us, length us, event | category | flops | bytes accessed | tf_op | source)
XLA Modules:
  0.0 20.1 jit_solution(10089445303773865397)
XLA Ops:
  0.0 19.3 %spectra_and_gradient.1 = (bf16[128,144]{1,0:T(8,128)(2,1)S(1)}, bf16[144,128]{1,0:T(8,128)(2,1)S(1)}) custom-call(f32[128,128]{1,0:T(8,128)} %refs_0_.1, s32[128,128]{1,0:T(8,128)} %refs_1_.1, f32[8,12,2,576]{3,2,1,0:T(2,128)} %bitcast.1, s32[2]{0:T(128)} %refs_3_.1, f32[8]{0:T(128)} %refs_4_.1, bf16[120,384]{1,0:T(8,128)(2,1)} %constant.32.clone.refs_5_, ...), custom_call_target="tpu_custom_call" | custom-call | tf_op jit(solution)/shard_map/spectra_and_gradient/pallas_call | solution.py:396
  19.3 0.8 %to_pixels.1 = f32[128,128]{1,0:T(8,128)} custom-call(bf16[128,144]{1,0:T(8,128)(2,1)S(1)} %get-tuple-element.7.table_ref, bf16[144,128]{1,0:T(8,128)(2,1)S(1)} %get-tuple-element.8.sums_ref), custom_call_target="tpu_custom_call" | custom-call | tf_op jit(solution)/shard_map/to_pixels/pallas_call | solution.py:421

commit v4 on v3

--- a/solution.py
+++ b/solution.py
@@ -24,8 +24,10 @@
 PACK = 5
 GRID = 48
 GROUP = 4
-CONDS = 2
-TILES = CONDS * KERNELS // GROUP
+CONDS = 4
+OWN = 2
+PER_COND = KERNELS // GROUP
+SLABS = 2 * OWN * PER_COND
 STEEP = 4.0
 THRESH = 0.6
 OFFSETS = [(-1, -1), (-1, 1), (0, -1), (-1, 0), (1, 0), (0, 1), (1, -1), (1, 1)]
@@ -171,7 +173,7 @@
     table_ref, out_ref = refs[5 + n : 7 + n]
     scratch = refs[7 + n :]
     tab = dict(zip(NAMES, list(scratch[: n - 1]) + [table_ref]))
-    mask, target, kernels, cond_ref, dose_ref, kk, sent, held, swap, load_sem, send_sem, recv_sem = scratch[n - 1 :]
+    mask, target, kernels, cond_ref, dose_ref, kk, sent, held, load_sem, send_sem, recv_sem = scratch[n - 1 :]
 
     row, col, core = (lax.axis_index(a) for a in ("row", "col", "cond"))
     n_row, n_col = lax.axis_size("row"), lax.axis_size("col")
@@ -189,19 +191,29 @@
         copies[name].start()
 
     held[...] = jnp.zeros_like(held)
+    even = lax.rem(col, 2) == 0
+
+    def from_core(dr, dc, at_row, at_col, at_core):
+        return jnp.where((at_row == 0) & (at_col == 0) & (at_core == 0), 0, 1) if dc else 0
+
     barrier = pltpu.get_barrier_semaphore()
     pl.semaphore_signal(barrier, inc=1, device_id=(row, col, 1 - core), device_id_type=MESH)
     there = []
     count = jnp.int32(1)
     for dr, dc in OFFSETS:
         ok = (row + dr >= 0) & (row + dr < n_row) & (col + dc >= 0) & (col + dc < n_col)
-        sender = 0 if dc == 0 else 1
         there.append(ok)
-        count = count + jnp.where(ok & (core == sender), 2, 0)
+        for to in range(2):
+            count = count + jnp.where(ok & (core == from_core(dr, dc, row + dr, col + dc, to)), 1, 0)
+        sender = from_core(dr, dc, row, col, core)
 
         @pl.when(ok)
         def _():
             pl.semaphore_signal(barrier, inc=1, device_id=(row + dr, col + dc, sender), device_id_type=MESH)
+
+    def sending(i, to):
+        dr, dc = OFFSETS[i]
+        return there[len(OFFSETS) - 1 - i] & (core == from_core(dr, dc, row - dr, col - dc, to))
 
     for name in ("mask", "dft_rows", "dft_cols"):
         copies[name].wait()
@@ -229,28 +241,26 @@
     def send(order):
         for i in order:
             dr, dc = OFFSETS[i]
-            for target in range(2):
-                sends[i, target] = pltpu.make_async_remote_copy(
+            for to in range(2):
+                sends[i, to] = pltpu.make_async_remote_copy(
                     src_ref=sent.at[i],
                     dst_ref=held.at[i],
-                    send_sem=send_sem.at[2 * i + target],
+                    send_sem=send_sem.at[2 * i + to],
                     recv_sem=recv_sem.at[i],
-                    device_id=(row - dr, col - dc, target),
+                    device_id=(row - dr, col - dc, to),
                     device_id_type=MESH,
                 )
 
-                @pl.when(there[len(OFFSETS) - 1 - i] & (core == (0 if dc == 0 else 1)))
+                @pl.when(sending(i, to))
                 def _():
-                    sends[i, target].start()
+                    sends[i, to].start()
 
     blocks_of(0)
-    ahead = jnp.where(lax.rem(col, 2) == 0, TILES, 0)
-
     lane = lax.broadcasted_iota(jnp.int32, (BAND, TILE), 1) // 32
 
     def arrange(step, carry):
-        c = step // 3
-        group = step - 3 * c
+        c = step // PER_COND
+        group = step - PER_COND * c
         setting = cond_ref[c]
         for part in range(2):
             total = jnp.zeros((BAND, TILE), F32)
@@ -259,16 +269,19 @@
                 high, low = split(line * tab["rows_of"][...])
                 folded = dot(high, tab["fold"][...]) + dot(low, tab["fold"][...])
                 total = total + jnp.where(lane == k, folded, 0.0)
-            kk[part, step] = total
+            kk[0, OWN * PER_COND * part + step] = total
         return carry
 
-    @pl.when(ahead > 0)
-    def _():
+    def arrange_all():
         for name, _, _ in later:
             copies[name].start()
         for name in LOADS:
             copies[name].wait()
-        lax.fori_loop(0, TILES, arrange, 0)
+        for c in range(OWN):
+            kk[0, SLABS, c : c + 1] = jnp.full((1, TILE), dose_ref[cond_ref[c]], F32)
+        lax.fori_loop(0, OWN * PER_COND, arrange, 0)
+
+    pl.when(even)(arrange_all)
 
     pl.semaphore_wait(barrier, count)
     send(ORDER[0])
@@ -277,17 +290,20 @@
     own = blocks_of(1)
     send(ORDER[2])
 
-    @pl.when(ahead == 0)
-    def _():
-        for name, _, _ in later:
-            copies[name].start()
-        for name in LOADS:
-            copies[name].wait()
-        lax.fori_loop(0, TILES, arrange, 0)
+    pl.when(jnp.logical_not(even))(arrange_all)
+    share = pltpu.make_async_remote_copy(
+        src_ref=kk.at[0],
+        dst_ref=kk.at[1],
+        send_sem=send_sem.at[2 * len(OFFSETS)],
+        recv_sem=recv_sem.at[len(OFFSETS)],
+        device_id=(row, col, 1 - core),
+        device_id_type=MESH,
+    )
+    share.start()
 
     for name in NAMES[4:] + ["target"]:
         copies[name].wait()
-    doses = [dose_ref[cond_ref[c]] for c in range(CONDS)]
+    share.wait_recv()
     goal = target[...].astype(F32)
 
     for i in range(len(OFFSETS)):
@@ -307,15 +323,20 @@
     high, low = split(chosen)
     spectrum = dot(high, tab["spread"][...]) + dot(low, tab["spread"][...])
     s_re, s_im = spectrum[:, :TILE], spectrum[:, TILE:]
+
+    def kernel_tile(j):
+        who, at = divmod(j, OWN * PER_COND)
+        return kk[who, at], kk[who, OWN * PER_COND + at]
+
     product = []
-    for j in range(TILES):
-        k_re, k_im = kk[0, j], kk[1, j]
+    for j in range(CONDS * PER_COND):
+        k_re, k_im = kernel_tile(j)
         product.append(jnp.concatenate([k_re * s_re - k_im * s_im, k_re * s_im + k_im * s_re], axis=0))
     along = dot(tab["field_rows"][...], stacked3(jnp.concatenate(product, axis=1)))
     along = jnp.concatenate(
         [
             jnp.concatenate([along[:GRID, TILE * j : TILE * (j + 1)], along[GRID:, TILE * j : TILE * (j + 1)]], axis=1)
-            for j in range(TILES)
+            for j in range(CONDS * PER_COND)
         ],
         axis=0,
     )
@@ -324,64 +345,52 @@
     square = square[:, : 2 * TILE] + square[:, 2 * TILE :]
     samples = []
     for c in range(CONDS):
-        at = c * (TILES // CONDS) * GRID
+        at = c * PER_COND * GRID
         samples.append(square[at : at + GRID] + square[at + GRID : at + 2 * GRID] + square[at + 2 * GRID : at + 3 * GRID])
     inten = dot3(jnp.concatenate(samples, axis=0), tab["inter_cols"])
-    inten = jnp.concatenate([inten[:GRID], inten[GRID:]], axis=1)
+    inten = jnp.concatenate([inten[GRID * c : GRID * (c + 1)] for c in range(CONDS)], axis=1)
     inten = dot(tab["inter_rows"][...], stacked3(inten))
     slopes = []
     for c in range(CONDS):
-        scale = doses[c] * (STEEP / (KERNELS * BAND * BAND))
+        scale = kk[c // OWN, SLABS, c % OWN : c % OWN + 1] * (STEEP / (KERNELS * BAND * BAND))
         arg = scale * inten[:, TILE * c : TILE * (c + 1)] - STEEP * THRESH
         e = jnp.exp(-jnp.abs(arg))
         inverse = 1.0 / (1.0 + e)
         resist = jnp.where(arg >= 0, inverse, e * inverse)
         slopes.append((resist - goal) * (e * inverse * inverse) * (4.0 * scale))
     back = dot(tab["inter_rows_t"][...], stacked3(jnp.concatenate(slopes, axis=1)))
-    back = jnp.concatenate([back[:, :TILE], back[:, TILE:]], axis=0)
+    back = jnp.concatenate([back[:, TILE * c : TILE * (c + 1)] for c in range(CONDS)], axis=0)
     weight = dot3(back, tab["inter_cols_t"])
     pulled = []
-    for j in range(TILES):
-        at = j // (TILES // CONDS) * GRID
+    for j in range(CONDS * PER_COND):
+        at = j // PER_COND * GRID
         w = weight[at : at + GRID]
         pulled.append(field[GRID * j : GRID * (j + 1)] * jnp.concatenate([w, w], axis=1))
     pulled = dot3(jnp.concatenate(pulled, axis=0), tab["field_cols_t"])
     pulled = jnp.concatenate(
         [
-            jnp.concatenate([pulled[GRID * j : GRID * (j + 1), TILE * p : TILE * (p + 1)] for j in range(TILES)], axis=1)
+            jnp.concatenate([pulled[GRID * j : GRID * (j + 1), TILE * p : TILE * (p + 1)] for j in range(CONDS * PER_COND)], axis=1)
             for p in range(2)
         ],
         axis=0,
     )
     pulled = dot(tab["field_rows_t"][...], stacked3(pulled))
     d_re = d_im = None
-    for j in range(TILES):
-        k_re, k_im = kk[0, j], kk[1, j]
+    for j in range(CONDS * PER_COND):
+        k_re, k_im = kernel_tile(j)
         p_re = pulled[:BAND, TILE * j : TILE * (j + 1)]
         p_im = pulled[BAND:, TILE * j : TILE * (j + 1)]
         re, im = k_re * p_re + k_im * p_im, k_re * p_im - k_im * p_re
         d_re, d_im = (re, im) if d_re is None else (d_re + re, d_im + im)
     last = dot3(jnp.concatenate([d_re, d_im], axis=1), tab["last_cols"])
-    swap[0, :BAND] = last[:, :TILE]
-    swap[0, BAND:] = last[:, TILE:]
-    copy = pltpu.make_async_remote_copy(
-        src_ref=swap.at[0],
-        dst_ref=swap.at[1],
-        send_sem=send_sem.at[2 * len(OFFSETS)],
-        recv_sem=recv_sem.at[len(OFFSETS)],
-        device_id=(row, col, 1 - core),
-        device_id_type=MESH,
-    )
-    copy.start()
-    for i, (dr, dc) in enumerate(OFFSETS):
-
-        @pl.when(there[len(OFFSETS) - 1 - i] & (core == (0 if dc == 0 else 1)))
-        def _(i=i):
-            for target in range(2):
-                sends[i, target].wait_send()
-
-    copy.wait()
-    out_ref[...] = stacked3(swap[0] + swap[1])
+    out_ref[...] = stacked3(jnp.concatenate([last[:, :TILE], last[:, TILE:]], axis=0))
+    share.wait_send()
+    for i in range(len(OFFSETS)):
+        for to in range(2):
+
+            @pl.when(sending(i, to))
+            def _(i=i, to=to):
+                sends[i, to].wait_send()
 
 
 def last_kernel(table_ref, sums_ref, out_ref):
@@ -405,10 +414,9 @@
             pltpu.VMEM(by_kernel.shape, F32),
             pltpu.SMEM(cond_index.shape, jnp.int32),
             pltpu.SMEM(dose.shape, F32),
-            pltpu.VMEM((2, TILES, BAND, TILE), F32),
+            pltpu.VMEM((2, SLABS + 1, BAND, TILE), F32),
             pltpu.VMEM((len(OFFSETS), PACK, TILE), F32),
             pltpu.VMEM((len(OFFSETS), PACK, TILE), F32),
-            pltpu.VMEM((2, 2 * BAND, TILE), F32),
             pltpu.SemaphoreType.DMA((len(tables) + 5,)),
             pltpu.SemaphoreType.DMA((2 * len(OFFSETS) + 1,)),
             pltpu.SemaphoreType.DMA((len(OFFSETS) + 1,)),

time: 20.2 us -> 18.9 us (0.936)
  Pallas kernels: 20.1 us -> 18.8 us
    pallas_call x1, Pallas kernels: 19.3 us -> 18 us  [shards(): pl.pallas_call(main_kernel, out_shape=[pltpu.VMEM(tables[-1].shape, BF),...]
where the time goes in v4:
time: 18.9 us; the launch traced here: 18.8 us
  Pallas kernels  18.8 us (99%)
    pallas_call x1, Pallas kernels, shards(): pl.pallas_call(main_kernel, out_shape=[pltpu.VMEM(tables[-1].shape, BF),...  18 us
    pallas_call x1, Pallas kernels, shards(): pl.pallas_call(last_kernel, out_shape=jax.ShapeDtypeStruct(mask.shape, F3...  0.78 us

profile of v4, /device:TPU:1, one launch (start us, length us, event | category | flops | bytes accessed | tf_op | source)
XLA Modules:
  0.0 18.8 jit_solution(10885696061470281592)
XLA Ops:
  0.0 18.0 %spectra_and_gradient.1 = (bf16[128,144]{1,0:T(8,128)(2,1)S(1)}, bf16[144,128]{1,0:T(8,128)(2,1)S(1)}) custom-call(f32[128,128]{1,0:T(8,128)} %refs_0_.1, s32[128,128]{1,0:T(8,128)} %refs_1_.1, f32[8,12,2,576]{3,2,1,0:T(2,128)} %bitcast.1, s32[2]{0:T(128)} %refs_3_.1, f32[8]{0:T(128)} %refs_4_.1, bf16[120,384]{1,0:T(8,128)(2,1)} %constant.32.clone.refs_5_, ...), custom_call_target="tpu_custom_call" | custom-call | tf_op jit(solution)/shard_map/spectra_and_gradient/pallas_call | solution.py:405
  18.0 0.8 %to_pixels.1 = f32[128,128]{1,0:T(8,128)} custom-call(bf16[128,144]{1,0:T(8,128)(2,1)S(1)} %get-tuple-element.7.table_ref, bf16[144,128]{1,0:T(8,128)(2,1)S(1)} %get-tuple-element.8.sums_ref), custom_call_target="tpu_custom_call" | custom-call | tf_op jit(solution)/shard_map/to_pixels/pallas_call | solution.py:429

commit v5 on v4

--- a/solution.py
+++ b/solution.py
@@ -161,6 +161,11 @@
     return dot(high, table[0]) + dot(low, table[0]) + dot(high, table[1])
 
 
+def dot3_in(pieces, x, table):
+    rows = x.shape[0] // pieces
+    return jnp.concatenate([dot3(x[rows * i : rows * (i + 1)], table) for i in range(pieces)], axis=0)
+
+
 def stacked3(x):
     high, low = split(x)
     return jnp.concatenate([high, low, high], axis=0)
@@ -347,7 +352,7 @@
     for c in range(CONDS):
         at = c * PER_COND * GRID
         samples.append(square[at : at + GRID] + square[at + GRID : at + 2 * GRID] + square[at + 2 * GRID : at + 3 * GRID])
-    inten = dot3(jnp.concatenate(samples, axis=0), tab["inter_cols"])
+    inten = dot3_in(2, jnp.concatenate(samples, axis=0), tab["inter_cols"])
     inten = jnp.concatenate([inten[GRID * c : GRID * (c + 1)] for c in range(CONDS)], axis=1)
     inten = dot(tab["inter_rows"][...], stacked3(inten))
     slopes = []
@@ -360,13 +365,13 @@
         slopes.append((resist - goal) * (e * inverse * inverse) * (4.0 * scale))
     back = dot(tab["inter_rows_t"][...], stacked3(jnp.concatenate(slopes, axis=1)))
     back = jnp.concatenate([back[:, TILE * c : TILE * (c + 1)] for c in range(CONDS)], axis=0)
-    weight = dot3(back, tab["inter_cols_t"])
+    weight = dot3_in(2, back, tab["inter_cols_t"])
     pulled = []
     for j in range(CONDS * PER_COND):
         at = j // PER_COND * GRID
         w = weight[at : at + GRID]
         pulled.append(field[GRID * j : GRID * (j + 1)] * jnp.concatenate([w, w], axis=1))
-    pulled = dot3(jnp.concatenate(pulled, axis=0), tab["field_cols_t"])
+    pulled = dot3_in(2, jnp.concatenate(pulled, axis=0), tab["field_cols_t"])
     pulled = jnp.concatenate(
         [
             jnp.concatenate([pulled[GRID * j : GRID * (j + 1), TILE * p : TILE * (p + 1)] for j in range(CONDS * PER_COND)], axis=1)

time: 18.9 us -> 18 us (0.952)
  Pallas kernels: 18.8 us -> 17.9 us
    pallas_call x1, Pallas kernels: 18 us -> 17.1 us  [shards(): pl.pallas_call(main_kernel, out_shape=[pltpu.VMEM(tables[-1].shape, BF),...]
where the time goes in v5:
time: 18 us; the launch traced here: 17.9 us
  Pallas kernels  17.9 us (99%)
    pallas_call x1, Pallas kernels, shards(): pl.pallas_call(main_kernel, out_shape=[pltpu.VMEM(tables[-1].shape, BF),...  17.1 us
    pallas_call x1, Pallas kernels, shards(): pl.pallas_call(last_kernel, out_shape=jax.ShapeDtypeStruct(mask.shape, F3...  0.78 us

profile of v5, /device:TPU:1, one launch (start us, length us, event | category | flops | bytes accessed | tf_op | source)
XLA Modules:
  0.0 17.9 jit_solution(16733138312458083280)
XLA Ops:
  0.0 17.1 %spectra_and_gradient.1 = (bf16[128,144]{1,0:T(8,128)(2,1)S(1)}, bf16[144,128]{1,0:T(8,128)(2,1)S(1)}) custom-call(f32[128,128]{1,0:T(8,128)} %refs_0_.1, s32[128,128]{1,0:T(8,128)} %refs_1_.1, f32[8,12,2,576]{3,2,1,0:T(2,128)} %bitcast.1, s32[2]{0:T(128)} %refs_3_.1, f32[8]{0:T(128)} %refs_4_.1, bf16[120,384]{1,0:T(8,128)(2,1)} %constant.32.clone.refs_5_, ...), custom_call_target="tpu_custom_call" | custom-call | tf_op jit(solution)/shard_map/spectra_and_gradient/pallas_call | solution.py:410
  17.1 0.8 %to_pixels.1 = f32[128,128]{1,0:T(8,128)} custom-call(bf16[128,144]{1,0:T(8,128)(2,1)S(1)} %get-tuple-element.7.table_ref, bf16[144,128]{1,0:T(8,128)(2,1)S(1)} %get-tuple-element.8.sums_ref), custom_call_target="tpu_custom_call" | custom-call | tf_op jit(solution)/shard_map/to_pixels/pallas_call | solution.py:434

commit v6 on v5

--- a/solution.py
+++ b/solution.py
@@ -32,6 +32,7 @@
 THRESH = 0.6
 OFFSETS = [(-1, -1), (-1, 1), (0, -1), (-1, 0), (1, 0), (0, 1), (1, -1), (1, 1)]
 ORDER = [(0, 6, 2), (1, 7, 5), (3, 4)]
+ARRIVAL = [3, 4, 5, 1, 7, 2, 0, 6]
 FREQ = np.arange(BAND) - HALF
 UNIT = 2.0 * math.pi / WINDOW
 
@@ -66,8 +67,9 @@
         rows[d, :, :PACK] = basis.reshape(PACK, PACK, TILE)
         for j in range(PACK):
             cols[d, :, REAL * j : REAL * (j + 1)] = basis.T / WINDOW
-    t["dft_rows"] = left3(rows.reshape(3 * PACK * 8, TILE))
-    t["dft_cols"] = pair(cols.transpose(1, 0, 2).reshape(TILE, 3 * TILE))
+    t["dft_rows"] = pair(rows.reshape(3 * PACK * 8, TILE))
+    for d in range(3):
+        t[f"dft_cols{d}"] = pair(cols[d])
 
     pick = np.zeros((PACK, BAND, 2 * TILE), np.float32)
     spread = np.zeros((2, TILE, 2, GROUP, 32))
@@ -139,7 +141,7 @@
 
 TABLES = make_tables()
 NAMES = [
-    "dft_rows", "dft_cols", "rows_of", "fold", "pick", "spread", "field_rows", "field_cols",
+    "dft_rows", "dft_cols0", "dft_cols2", "dft_cols1", "rows_of", "fold", "pick", "spread", "field_rows", "field_cols",
     "inter_cols", "inter_rows", "inter_rows_t", "inter_cols_t", "field_cols_t", "field_rows_t", "last_cols",
     "last_rows",
 ]
@@ -184,10 +186,10 @@
     n_row, n_col = lax.axis_size("row"), lax.axis_size("col")
 
     copies = {}
-    first = [("mask", mask_hbm, mask)] + [(m, s, tab[m]) for m, s in zip(NAMES[:2], tables_hbm[:2])]
+    first = [("mask", mask_hbm, mask)] + [(m, s, tab[m]) for m, s in zip(NAMES[:4], tables_hbm[:4])]
     later = (
         [("kernels", kernels_hbm, kernels), ("cond", cond_hbm, cond_ref), ("dose", dose_hbm, dose_ref)]
-        + [(m, s, tab[m]) for m, s in zip(NAMES[2:], tables_hbm[2:])]
+        + [(m, s, tab[m]) for m, s in zip(NAMES[4:], tables_hbm[4:])]
         + [("target", target_hbm, target)]
     )
     for i, (name, src, dst) in enumerate(first + later):
@@ -220,14 +222,16 @@
         dr, dc = OFFSETS[i]
         return there[len(OFFSETS) - 1 - i] & (core == from_core(dr, dc, row - dr, col - dc, to))
 
-    for name in ("mask", "dft_rows", "dft_cols"):
+    for name in ("mask", "dft_rows"):
         copies[name].wait()
     lanes = lax.broadcasted_iota(jnp.int32, (8, TILE), 1)
-    partial = dot(tab["dft_rows"][...], stacked3(mask[...]))
+    table = tab["dft_rows"]
+    partial = dot(jnp.concatenate([table[0], table[0], table[1]], axis=1), stacked3(mask[...]))
     partial = split(partial)
 
     def blocks_of(e):
-        table = [tab["dft_cols"][p, :, TILE * e : TILE * (e + 1)] for p in range(2)]
+        copies[f"dft_cols{e}"].wait()
+        table = tab[f"dft_cols{e}"]
         products = dot(partial[0], table[0]) + dot(partial[1], table[0]) + dot(partial[0], table[1])
         own = None
         for d in range(3):
@@ -267,13 +271,15 @@
         c = step // PER_COND
         group = step - PER_COND * c
         setting = cond_ref[c]
+        lines = [kernels[setting, group * GROUP + k, part : part + 1, :] for part in range(2) for k in range(GROUP)]
+        folded = []
+        for half in (lines[:GROUP], lines[GROUP:]):
+            high, low = split(jnp.concatenate([line * tab["rows_of"][...] for line in half], axis=0))
+            folded.append(dot(high, tab["fold"][...]) + dot(low, tab["fold"][...]))
         for part in range(2):
-            total = jnp.zeros((BAND, TILE), F32)
-            for k in range(GROUP):
-                line = kernels[setting, group * GROUP + k, part : part + 1, :]
-                high, low = split(line * tab["rows_of"][...])
-                folded = dot(high, tab["fold"][...]) + dot(low, tab["fold"][...])
-                total = total + jnp.where(lane == k, folded, 0.0)
+            total = folded[part][:BAND]
+            for k in range(1, GROUP):
+                total = jnp.where(lane == k, folded[part][BAND * k : BAND * (k + 1)], total)
             kk[0, OWN * PER_COND * part + step] = total
         return carry
 
@@ -286,7 +292,8 @@
             kk[0, SLABS, c : c + 1] = jnp.full((1, TILE), dose_ref[cond_ref[c]], F32)
         lax.fori_loop(0, OWN * PER_COND, arrange, 0)
 
-    pl.when(even)(arrange_all)
+    ahead = even & ((row > 0) | (col > 0) | (core > 0))
+    pl.when(ahead)(arrange_all)
 
     pl.semaphore_wait(barrier, count)
     send(ORDER[0])
@@ -295,7 +302,7 @@
     own = blocks_of(1)
     send(ORDER[2])
 
-    pl.when(jnp.logical_not(even))(arrange_all)
+    pl.when(jnp.logical_not(ahead))(arrange_all)
     share = pltpu.make_async_remote_copy(
         src_ref=kk.at[0],
         dst_ref=kk.at[1],
@@ -306,19 +313,18 @@
     )
     share.start()
 
-    for name in NAMES[4:] + ["target"]:
+    for name in NAMES[6:] + ["target"]:
         copies[name].wait()
     share.wait_recv()
     goal = target[...].astype(F32)
 
-    for i in range(len(OFFSETS)):
+    z = own[:PACK]
+    for i in ARRIVAL:
 
         @pl.when(there[i])
         def _(i=i):
             sends[i, 0].wait_recv()
 
-    z = own[:PACK]
-    for i in range(len(OFFSETS)):
         z = z + held[i]
     chosen = None
     for i in range(PACK):

time: 18 us -> 17.8 us (0.989)
  Pallas kernels: 17.9 us -> 17.6 us
    pallas_call x1, Pallas kernels: 17.1 us -> 16.8 us  [shards(): pl.pallas_call(main_kernel, out_shape=[pltpu.VMEM(tables[-1].shape, BF),...]
where the time goes in v6:
time: 17.8 us; the launch traced here: 17.6 us
  Pallas kernels  17.6 us (99%)
    pallas_call x1, Pallas kernels, shards(): pl.pallas_call(main_kernel, out_shape=[pltpu.VMEM(tables[-1].shape, BF),...  16.8 us
    pallas_call x1, Pallas kernels, shards(): pl.pallas_call(last_kernel, out_shape=jax.ShapeDtypeStruct(mask.shape, F3...  0.78 us

profile of v6, /device:TPU:1, one launch (start us, length us, event | category | flops | bytes accessed | tf_op | source)
XLA Modules:
  0.0 17.6 jit_solution(1309870482364173855)
XLA Ops:
  0.0 16.8 %spectra_and_gradient.1 = (bf16[128,144]{1,0:T(8,128)(2,1)S(1)}, bf16[144,128]{1,0:T(8,128)(2,1)S(1)}) custom-call(f32[128,128]{1,0:T(8,128)} %refs_0_.1, s32[128,128]{1,0:T(8,128)} %refs_1_.1, f32[8,12,2,576]{3,2,1,0:T(2,128)} %bitcast.1, s32[2]{0:T(128)} %refs_3_.1, f32[8]{0:T(128)} %refs_4_.1, bf16[2,120,128]{2,1,0:T(8,128)(2,1)} %constant.36.clone.refs_5_, ...), custom_call_target="tpu_custom_call" | custom-call | tf_op jit(solution)/shard_map/spectra_and_gradient/pallas_call | solution.py:416
  16.8 0.8 %to_pixels.1 = f32[128,128]{1,0:T(8,128)} custom-call(bf16[128,144]{1,0:T(8,128)(2,1)S(1)} %get-tuple-element.7.table_ref, bf16[144,128]{1,0:T(8,128)(2,1)S(1)} %get-tuple-element.8.sums_ref), custom_call_target="tpu_custom_call" | custom-call | tf_op jit(solution)/shard_map/to_pixels/pallas_call | solution.py:440

commit v7 on v6

--- a/solution.py
+++ b/solution.py
@@ -67,7 +67,7 @@
         rows[d, :, :PACK] = basis.reshape(PACK, PACK, TILE)
         for j in range(PACK):
             cols[d, :, REAL * j : REAL * (j + 1)] = basis.T / WINDOW
-    t["dft_rows"] = pair(rows.reshape(3 * PACK * 8, TILE))
+    t["dft_rows"] = pair(np.pad(rows.reshape(3 * PACK * 8, TILE), ((0, 8), (0, 0))))
     for d in range(3):
         t[f"dft_cols{d}"] = pair(cols[d])
 

time: 17.8 us -> 17.8 us (level)
  no operation moved by 1% of the time
where the time goes in v7:
time: 17.8 us; the launch traced here: 17.6 us
  Pallas kernels  17.6 us (99%)
    pallas_call x1, Pallas kernels, shards(): pl.pallas_call(main_kernel, out_shape=[pltpu.VMEM(tables[-1].shape, BF),...  16.8 us
    pallas_call x1, Pallas kernels, shards(): pl.pallas_call(last_kernel, out_shape=jax.ShapeDtypeStruct(mask.shape, F3...  0.78 us

profile of v7, /device:TPU:1, one launch (start us, length us, event | category | flops | bytes accessed | tf_op | source)
XLA Modules:
  0.0 17.6 jit_solution(474965907300180320)
XLA Ops:
  0.0 16.8 %spectra_and_gradient.1 = (bf16[128,144]{1,0:T(8,128)(2,1)S(1)}, bf16[144,128]{1,0:T(8,128)(2,1)S(1)}) custom-call(f32[128,128]{1,0:T(8,128)} %refs_0_.1, s32[128,128]{1,0:T(8,128)} %refs_1_.1, f32[8,12,2,576]{3,2,1,0:T(2,128)} %bitcast.1, s32[2]{0:T(128)} %refs_3_.1, f32[8]{0:T(128)} %refs_4_.1, bf16[2,128,128]{2,1,0:T(8,128)(2,1)} %constant.36.clone.refs_5_, ...), custom_call_target="tpu_custom_call" | custom-call | tf_op jit(solution)/shard_map/spectra_and_gradient/pallas_call | solution.py:416
  16.8 0.8 %to_pixels.1 = f32[128,128]{1,0:T(8,128)} custom-call(bf16[128,144]{1,0:T(8,128)(2,1)S(1)} %get-tuple-element.7.table_ref, bf16[144,128]{1,0:T(8,128)(2,1)S(1)} %get-tuple-element.8.sums_ref), custom_call_target="tpu_custom_call" | custom-call | tf_op jit(solution)/shard_map/to_pixels/pallas_call | solution.py:440

commit v8 on v7

--- a/solution.py
+++ b/solution.py
@@ -317,6 +317,13 @@
         copies[name].wait()
     share.wait_recv()
     goal = target[...].astype(F32)
+
+    for i in range(len(OFFSETS)):
+        for to in range(2):
+
+            @pl.when(sending(i, to))
+            def _(i=i, to=to):
+                sends[i, to].wait_send()
 
     z = own[:PACK]
     for i in ARRIVAL:
@@ -396,12 +403,6 @@
     last = dot3(jnp.concatenate([d_re, d_im], axis=1), tab["last_cols"])
     out_ref[...] = stacked3(jnp.concatenate([last[:, :TILE], last[:, TILE:]], axis=0))
     share.wait_send()
-    for i in range(len(OFFSETS)):
-        for to in range(2):
-
-            @pl.when(sending(i, to))
-            def _(i=i, to=to):
-                sends[i, to].wait_send()
 
 
 def last_kernel(table_ref, sums_ref, out_ref):

time: 17.8 us -> 17.8 us (level)
  no operation moved by 1% of the time
where the time goes in v8:
time: 17.8 us; the launch traced here: 17.6 us
  Pallas kernels  17.6 us (99%)
    pallas_call x1, Pallas kernels, shards(): pl.pallas_call(main_kernel, out_shape=[pltpu.VMEM(tables[-1].shape, BF),...  16.8 us
    pallas_call x1, Pallas kernels, shards(): pl.pallas_call(last_kernel, out_shape=jax.ShapeDtypeStruct(mask.shape, F3...  0.78 us

profile of v8, /device:TPU:1, one launch (start us, length us, event | category | flops | bytes accessed | tf_op | source)
XLA Modules:
  0.0 17.6 jit_solution(464130921599432381)
XLA Ops:
  0.0 16.8 %spectra_and_gradient.1 = (bf16[128,144]{1,0:T(8,128)(2,1)S(1)}, bf16[144,128]{1,0:T(8,128)(2,1)S(1)}) custom-call(f32[128,128]{1,0:T(8,128)} %refs_0_.1, s32[128,128]{1,0:T(8,128)} %refs_1_.1, f32[8,12,2,576]{3,2,1,0:T(2,128)} %bitcast.1, s32[2]{0:T(128)} %refs_3_.1, f32[8]{0:T(128)} %refs_4_.1, bf16[2,128,128]{2,1,0:T(8,128)(2,1)} %constant.36.clone.refs_5_, ...), custom_call_target="tpu_custom_call" | custom-call | tf_op jit(solution)/shard_map/spectra_and_gradient/pallas_call | solution.py:417
  16.8 0.8 %to_pixels.1 = f32[128,128]{1,0:T(8,128)} custom-call(bf16[128,144]{1,0:T(8,128)(2,1)S(1)} %get-tuple-element.7.table_ref, bf16[144,128]{1,0:T(8,128)(2,1)S(1)} %get-tuple-element.8.sums_ref), custom_call_target="tpu_custom_call" | custom-call | tf_op jit(solution)/shard_map/to_pixels/pallas_call | solution.py:441

commit v9 on v8

--- a/solution.py
+++ b/solution.py
@@ -222,6 +222,8 @@
         dr, dc = OFFSETS[i]
         return there[len(OFFSETS) - 1 - i] & (core == from_core(dr, dc, row - dr, col - dc, to))
 
+    goes = {(i, to): sending(i, to) for i in range(len(OFFSETS)) for to in range(2)}
+
     for name in ("mask", "dft_rows"):
         copies[name].wait()
     lanes = lax.broadcasted_iota(jnp.int32, (8, TILE), 1)
@@ -260,7 +262,7 @@
                     device_id_type=MESH,
                 )
 
-                @pl.when(sending(i, to))
+                @pl.when(goes[i, to])
                 def _():
                     sends[i, to].start()
 
@@ -321,7 +323,7 @@
     for i in range(len(OFFSETS)):
         for to in range(2):
 
-            @pl.when(sending(i, to))
+            @pl.when(goes[i, to])
             def _(i=i, to=to):
                 sends[i, to].wait_send()
 

time: 17.8 us -> 17.8 us (level)
  no operation moved by 1% of the time
where the time goes in v9:
time: 17.8 us; the launch traced here: 17.6 us
  Pallas kernels  17.6 us (99%)
    pallas_call x1, Pallas kernels, shards(): pl.pallas_call(main_kernel, out_shape=[pltpu.VMEM(tables[-1].shape, BF),...  16.8 us
    pallas_call x1, Pallas kernels, shards(): pl.pallas_call(last_kernel, out_shape=jax.ShapeDtypeStruct(mask.shape, F3...  0.78 us

profile of v9, /device:TPU:1, one launch (start us, length us, event | category | flops | bytes accessed | tf_op | source)
XLA Modules:
  0.0 17.6 jit_solution(464130921599432381)
XLA Ops:
  0.0 16.8 %spectra_and_gradient.1 = (bf16[128,144]{1,0:T(8,128)(2,1)S(1)}, bf16[144,128]{1,0:T(8,128)(2,1)S(1)}) custom-call(f32[128,128]{1,0:T(8,128)} %refs_0_.1, s32[128,128]{1,0:T(8,128)} %refs_1_.1, f32[8,12,2,576]{3,2,1,0:T(2,128)} %bitcast.1, s32[2]{0:T(128)} %refs_3_.1, f32[8]{0:T(128)} %refs_4_.1, bf16[2,128,128]{2,1,0:T(8,128)(2,1)} %constant.36.clone.refs_5_, ...), custom_call_target="tpu_custom_call" | custom-call | tf_op jit(solution)/shard_map/spectra_and_gradient/pallas_call | solution.py:419
  16.8 0.8 %to_pixels.1 = f32[128,128]{1,0:T(8,128)} custom-call(bf16[128,144]{1,0:T(8,128)(2,1)S(1)} %get-tuple-element.7.table_ref, bf16[144,128]{1,0:T(8,128)(2,1)S(1)} %get-tuple-element.8.sums_ref), custom_call_target="tpu_custom_call" | custom-call | tf_op jit(solution)/shard_map/to_pixels/pallas_call | solution.py:443
